TPU v7x, 32 devices: a whole 2x2x4 slice. The times are simulated.
32 devices in a mesh: dp: 2 (over core), fsdp: 16 (over z, y, x).
Axes of the slice: x: 2, y: 2, z: 4, core: 2. Of those that a mesh axis runs over, the one named last changes fastest.
Arguments:
- tokens: bfloat16 [64, 512, 768], P(('dp', 'fsdp')), may hold values from -6 to 6
- lengths: int32 [64], P(('dp', 'fsdp')), may hold values from 65 to 512, as said below
- query_key_value_weight: bfloat16 [768, 2304], P('fsdp'), may hold values from -0.21875 to 0.21875
- qv_bias: bfloat16 [1536], P('fsdp'), may hold values from -3 to 3
- output_projection_weight: bfloat16 [768, 768], P('fsdp'), may hold values from -0.875 to 0.875
- output_projection_bias: bfloat16 [768], P('fsdp'), may hold values from -3 to 3
- gain_one: bfloat16 [768], P('fsdp'), may hold values from 0.25 to 1.75
- shift_one: bfloat16 [768], P('fsdp'), may hold values from -2 to 2
- widening_matrix: bfloat16 [768, 3072], P('fsdp'), may hold values from -0.21875 to 0.21875
- widening_offset_vector: bfloat16 [3072], P('fsdp'), may hold values from -3 to 3
- down_projection_weight: bfloat16 [3072, 768], P('fsdp'), may hold values from -0.109375 to 0.109375
- down_projection_bias: bfloat16 [768], P('fsdp'), may hold values from -2 to 2
- gain_two: bfloat16 [768], P('fsdp'), may hold values from 0.25 to 1.75
- shift_two: bfloat16 [768], P('fsdp'), may hold values from -2 to 2
- cotangent: bfloat16 [64, 512, 768], P(('dp', 'fsdp')), may hold values from -6 to 6
Outputs:
- output: bfloat16 [64, 512, 768], P(('dp', 'fsdp'))
- grad_tokens: bfloat16 [64, 512, 768], P(('dp', 'fsdp'))
- grad_qkv_weight: float32 [768, 2304], P('fsdp')
- grad_qv_bias: float32 [1536], P('fsdp')
- grad_out_weight: float32 [768, 768], P('fsdp')
- grad_out_bias: float32 [768], P('fsdp')
- grad_gain_one: float32 [768], P('fsdp')
- grad_shift_one: float32 [768], P('fsdp')
- grad_up_weight: float32 [768, 3072], P('fsdp')
- grad_up_bias: float32 [3072], P('fsdp')
- grad_down_weight: float32 [3072, 768], P('fsdp')
- grad_down_bias: float32 [768], P('fsdp')
- grad_gain_two: float32 [768], P('fsdp')
- grad_shift_two: float32 [768], P('fsdp')
Inputs may be any that keep to these rules, and one draw needn't show every extreme that they name: `lengths`: each length lies in the upper half of one of the bucket sizes 512/4, 256 and 512; some sequence has length 512.
All inputs are finite; a program needn't handle non-finite values.
Results may differ from a plain program's by a relative error of at most 0.015.
Values may be sent and summed in bfloat16 or wider, within the bound.
No kernel may reach another device: no remote copies, remote signals or barrier semaphores. Data moves between devices by JAX's collectives and lax.ppermute only.
A program may use at most 192 MiB of HBM per device.

v0:
```python
import jax
import jax.numpy as jnp
from jax import lax
from jax.sharding import PartitionSpec as P

HEAD_DIM = 64


EPSILON = 1e-12
MASKED = -1e30


def norm_parts(values):
    centred = values - jnp.mean(values, axis=-1, keepdims=True)
    inv_root = lax.rsqrt(jnp.mean(centred * centred, axis=-1, keepdims=True) + EPSILON)
    return (centred * inv_root, inv_root)


def norm_back(grad_in, standard, inv_root, gain_vec):
    scaled = grad_in * gain_vec
    return inv_root * (
        scaled
        - jnp.mean(scaled, axis=-1, keepdims=True)
        - standard * jnp.mean(scaled * standard, axis=-1, keepdims=True)
    )


def gelu_exact(values):
    return 0.5 * values * (1.0 + lax.erf(values * 0.7071067811865476))


def gelu_slope(values):
    return (
        0.5 * (1.0 + lax.erf(values * 0.7071067811865476))
        + values * jnp.exp(-0.5 * values * values) * 0.3989422804014327
    )


def attention_scores(residual_mixed, key_valid):
    raw_scores = (
        jnp.einsum(
            "sqhc,skhc->shqk",
            residual_mixed[:, :, 0],
            residual_mixed[:, :, 1],
            preferred_element_type=jnp.float32,
        )
        * 0.125
    )
    return jnp.where(key_valid[:, None, None, :], raw_scores, MASKED)


def shards(
    tokens,
    lengths,
    query_key_value_weight,
    qv_bias,
    output_projection_weight,
    output_projection_bias,
    gain_one,
    shift_one,
    widening_matrix,
    widening_offset_vector,
    down_projection_weight,
    down_projection_bias,
    gain_two,
    shift_two,
    cotangent,
):
    seq_count, seq_length, model_width = tokens.shape
    row_count = seq_count * seq_length
    head_count = model_width // HEAD_DIM
    attn_set = (
        lax.all_gather(query_key_value_weight, "fsdp", axis=0, tiled=True),
        lax.all_gather(qv_bias, "fsdp", axis=0, tiled=True),
        lax.all_gather(output_projection_weight, "fsdp", axis=0, tiled=True),
        lax.all_gather(output_projection_bias, "fsdp", axis=0, tiled=True),
        lax.all_gather(gain_one, "fsdp", axis=0, tiled=True),
        lax.all_gather(shift_one, "fsdp", axis=0, tiled=True),
    )
    ffn_set = (
        lax.all_gather(widening_matrix, "fsdp", axis=0, tiled=True),
        lax.all_gather(widening_offset_vector, "fsdp", axis=0, tiled=True),
        lax.all_gather(down_projection_weight, "fsdp", axis=0, tiled=True),
        lax.all_gather(down_projection_bias, "fsdp", axis=0, tiled=True),
        lax.all_gather(gain_two, "fsdp", axis=0, tiled=True),
        lax.all_gather(shift_two, "fsdp", axis=0, tiled=True),
    )
    full_qkv, full_qv, full_out, full_out_bias, full_gain_one, full_shift_one = attn_set
    full_up, full_up_bias, full_down, full_down_bias, full_gain_two, full_shift_two = ffn_set
    flat_tokens = tokens.reshape(row_count, model_width)
    key_valid = jnp.arange(seq_length)[None, :] < lengths[:, None]
    qv_float = full_qv.astype(jnp.float32)
    every_bias = jnp.concatenate(
        [qv_float[:model_width], jnp.zeros((model_width,), jnp.float32), qv_float[model_width:]]
    )
    residual_mixed = (
        jnp.dot(flat_tokens, full_qkv, preferred_element_type=jnp.float32) + every_bias
    ).astype(jnp.bfloat16)
    residual_mixed = residual_mixed.reshape(seq_count, seq_length, 3, head_count, HEAD_DIM)
    scores = attention_scores(residual_mixed, key_valid)
    row_top = jnp.max(scores, axis=-1, keepdims=True)
    exp_scores = jnp.exp(scores - row_top)
    row_total = jnp.sum(exp_scores, axis=-1, keepdims=True)
    log_total = row_top + jnp.log(row_total)
    softmax_low = (exp_scores / row_total).astype(jnp.bfloat16)
    attention_output = jnp.einsum(
        "shqk,skhc->sqhc", softmax_low, residual_mixed[:, :, 2], preferred_element_type=jnp.float32
    )
    attended_low = attention_output.reshape(row_count, model_width).astype(jnp.bfloat16)
    attention_branch = jnp.dot(
        attended_low, full_out, preferred_element_type=jnp.float32
    ) + full_out_bias.astype(jnp.float32)
    standard_one, root_one = norm_parts(flat_tokens.astype(jnp.float32) + attention_branch)
    normed_low = (
        standard_one * full_gain_one.astype(jnp.float32) + full_shift_one.astype(jnp.float32)
    ).astype(jnp.bfloat16)
    hidden_before_gelu = jnp.dot(
        normed_low, full_up, preferred_element_type=jnp.float32
    ) + full_up_bias.astype(jnp.float32)
    active_low = gelu_exact(hidden_before_gelu).astype(jnp.bfloat16)
    feedforward_branch = jnp.dot(
        active_low, full_down, preferred_element_type=jnp.float32
    ) + full_down_bias.astype(jnp.float32)
    standard_two, root_two = norm_parts(normed_low.astype(jnp.float32) + feedforward_branch)
    output = (
        standard_two * full_gain_two.astype(jnp.float32) + full_shift_two.astype(jnp.float32)
    ).astype(jnp.bfloat16)
    back_qkv, back_out, back_gain_one = (
        lax.all_gather(query_key_value_weight, "fsdp", axis=0, tiled=True),
        lax.all_gather(output_projection_weight, "fsdp", axis=0, tiled=True),
        lax.all_gather(gain_one, "fsdp", axis=0, tiled=True),
    )
    back_up, back_down, back_gain_two = (
        lax.all_gather(widening_matrix, "fsdp", axis=0, tiled=True),
        lax.all_gather(down_projection_weight, "fsdp", axis=0, tiled=True),
        lax.all_gather(gain_two, "fsdp", axis=0, tiled=True),
    )
    out_grad = cotangent.reshape(row_count, model_width).astype(jnp.float32)
    grad_gain_two = jnp.sum(out_grad * standard_two, axis=0)
    grad_shift_two = jnp.sum(out_grad, axis=0)
    second_grad = norm_back(out_grad, standard_two, root_two, back_gain_two.astype(jnp.float32))
    branch_two_grad = second_grad.astype(jnp.bfloat16)
    grad_down_bias = jnp.sum(branch_two_grad.astype(jnp.float32), axis=0)
    grad_down_weight = jnp.einsum(
        "rf,rd->fd", active_low, branch_two_grad, preferred_element_type=jnp.float32
    )
    active_grad = jnp.einsum(
        "rd,fd->rf", branch_two_grad, back_down, preferred_element_type=jnp.float32
    )
    pre_grad = (active_grad * gelu_slope(hidden_before_gelu)).astype(jnp.bfloat16)
    grad_up_bias = jnp.sum(pre_grad.astype(jnp.float32), axis=0)
    grad_up_weight = jnp.einsum(
        "rd,rf->df", normed_low, pre_grad, preferred_element_type=jnp.float32
    )
    normed_grad = (
        jnp.einsum("rf,df->rd", pre_grad, back_up, preferred_element_type=jnp.float32) + second_grad
    )
    ffn_local = (
        lax.psum_scatter(grad_up_weight, "fsdp", scatter_dimension=0, tiled=True),
        lax.psum_scatter(grad_up_bias, "fsdp", scatter_dimension=0, tiled=True),
        lax.psum_scatter(grad_down_weight, "fsdp", scatter_dimension=0, tiled=True),
        lax.psum_scatter(grad_down_bias, "fsdp", scatter_dimension=0, tiled=True),
        lax.psum_scatter(grad_gain_two, "fsdp", scatter_dimension=0, tiled=True),
        lax.psum_scatter(grad_shift_two, "fsdp", scatter_dimension=0, tiled=True),
    )
    ffn_final = (
        lax.psum(ffn_local[0].astype(jnp.bfloat16), "dp").astype(jnp.float32),
        lax.psum(ffn_local[1].astype(jnp.bfloat16), "dp").astype(jnp.float32),
        lax.psum(ffn_local[2].astype(jnp.bfloat16), "dp").astype(jnp.float32),
        lax.psum(ffn_local[3].astype(jnp.bfloat16), "dp").astype(jnp.float32),
        lax.psum(ffn_local[4].astype(jnp.bfloat16), "dp").astype(jnp.float32),
        lax.psum(ffn_local[5].astype(jnp.bfloat16), "dp").astype(jnp.float32),
    )
    grad_gain_one = jnp.sum(normed_grad * standard_one, axis=0)
    grad_shift_one = jnp.sum(normed_grad, axis=0)
    first_grad = norm_back(normed_grad, standard_one, root_one, back_gain_one.astype(jnp.float32))
    branch_one_grad = first_grad.astype(jnp.bfloat16)
    grad_out_bias = jnp.sum(branch_one_grad.astype(jnp.float32), axis=0)
    grad_out_weight = jnp.einsum(
        "rd,re->de", attended_low, branch_one_grad, preferred_element_type=jnp.float32
    )
    attended_grad = jnp.einsum(
        "re,de->rd", branch_one_grad, back_out, preferred_element_type=jnp.float32
    )
    attended_grad = attended_grad.astype(jnp.bfloat16).reshape(
        seq_count, seq_length, head_count, HEAD_DIM
    )
    softmax_again = jnp.exp(attention_scores(residual_mixed, key_valid) - log_total)
    prob_grad = jnp.einsum(
        "sqhc,skhc->shqk",
        attended_grad,
        residual_mixed[:, :, 2],
        preferred_element_type=jnp.float32,
    )
    value_grad = jnp.einsum(
        "shqk,sqhc->skhc", softmax_low, attended_grad, preferred_element_type=jnp.float32
    )
    row_dot = jnp.sum(softmax_again * prob_grad, axis=-1, keepdims=True)
    score_grad = (softmax_again * (prob_grad - row_dot)).astype(jnp.bfloat16)
    query_grad = (
        jnp.einsum(
            "shqk,skhc->sqhc",
            score_grad,
            residual_mixed[:, :, 1],
            preferred_element_type=jnp.float32,
        )
        * 0.125
    )
    key_grad = (
        jnp.einsum(
            "shqk,sqhc->skhc",
            score_grad,
            residual_mixed[:, :, 0],
            preferred_element_type=jnp.float32,
        )
        * 0.125
    )
    mixed_grad = jnp.stack([query_grad, key_grad, value_grad], axis=2).astype(jnp.bfloat16)
    mixed_grad = mixed_grad.reshape(row_count, 3 * model_width)
    column_sums = jnp.sum(mixed_grad.astype(jnp.float32), axis=0)
    grad_qv_bias = jnp.concatenate([column_sums[:model_width], column_sums[2 * model_width :]])
    grad_qkv_weight = jnp.einsum(
        "rd,re->de", flat_tokens, mixed_grad, preferred_element_type=jnp.float32
    )
    grad_tokens = first_grad + jnp.einsum(
        "re,de->rd", mixed_grad, back_qkv, preferred_element_type=jnp.float32
    )
    grad_tokens = grad_tokens.astype(jnp.bfloat16).reshape(seq_count, seq_length, model_width)
    attn_local = (
        lax.psum_scatter(grad_qkv_weight, "fsdp", scatter_dimension=0, tiled=True),
        lax.psum_scatter(grad_qv_bias, "fsdp", scatter_dimension=0, tiled=True),
        lax.psum_scatter(grad_out_weight, "fsdp", scatter_dimension=0, tiled=True),
        lax.psum_scatter(grad_out_bias, "fsdp", scatter_dimension=0, tiled=True),
        lax.psum_scatter(grad_gain_one, "fsdp", scatter_dimension=0, tiled=True),
        lax.psum_scatter(grad_shift_one, "fsdp", scatter_dimension=0, tiled=True),
    )
    attn_final = (
        lax.psum(attn_local[0].astype(jnp.bfloat16), "dp").astype(jnp.float32),
        lax.psum(attn_local[1].astype(jnp.bfloat16), "dp").astype(jnp.float32),
        lax.psum(attn_local[2].astype(jnp.bfloat16), "dp").astype(jnp.float32),
        lax.psum(attn_local[3].astype(jnp.bfloat16), "dp").astype(jnp.float32),
        lax.psum(attn_local[4].astype(jnp.bfloat16), "dp").astype(jnp.float32),
        lax.psum(attn_local[5].astype(jnp.bfloat16), "dp").astype(jnp.float32),
    )
    computed_answers = tuple(attn_final) + tuple(ffn_final)
    return (
        output.reshape(seq_count, seq_length, model_width),
        grad_tokens,
        computed_answers[0],
        computed_answers[1],
        computed_answers[2],
        computed_answers[3],
        computed_answers[4],
        computed_answers[5],
        computed_answers[6],
        computed_answers[7],
        computed_answers[8],
        computed_answers[9],
        computed_answers[10],
        computed_answers[11],
    )


def solution(mesh):
    placed = (
        P(("dp", "fsdp"), None, None),
        P(("dp", "fsdp")),
        P("fsdp", None),
        P("fsdp"),
        P("fsdp", None),
        P("fsdp"),
        P("fsdp"),
        P("fsdp"),
        P("fsdp", None),
        P("fsdp"),
        P("fsdp", None),
        P("fsdp"),
        P("fsdp"),
        P("fsdp"),
        P(("dp", "fsdp"), None, None),
    )
    return jax.shard_map(
        shards,
        mesh=mesh,
        in_specs=placed,
        out_specs=(
            P(("dp", "fsdp"), None, None),
            P(("dp", "fsdp"), None, None),
            P("fsdp", None),
            P("fsdp"),
            P("fsdp", None),
            P("fsdp"),
            P("fsdp"),
            P("fsdp"),
            P("fsdp", None),
            P("fsdp"),
            P("fsdp", None),
            P("fsdp"),
            P("fsdp"),
            P("fsdp"),
        ),
        check_vma=False,
    )
```

profile of v0, /device:TPU:0, one launch (start us, length us, event | category | flops | bytes accessed | tf_op | source)
XLA Modules:
  0.0 1040.2 jit_solution(398960157404606943)
XLA Ops:
  10.0 1.3 fusion.30
  14.9 0.8 dynamic-update-slice.5
  15.7 0.8 dynamic-update-slice.2
  19.0 0.8 dynamic-update-slice
  19.9 0.8 dynamic-update-slice.4
  20.7 79.3 %all-reduce.17 = (bf16[1536]{0:T(1024)(128)(2,1)S(1)}, bf16[768]{0:T(1024)(128)(2,1)S(1)}, bf16[768]{0:T(1024)(128)(2,1)S(1)}, bf16[768]{0:T(1024)(128)(2,1)S(1)...) all-reduce(bf16[1536]{0:T(1024)(128)(2,1)S(1)} %dynamic-update-slic, ...), channel_id=1, replica_groups=mesh['dp'=2,'fsdp'=16] {'fsdp'}, use_global_device_ids=true, to_apply=%add | all-reduce | flops 9216 | bytes 36864
  100.1 2.7 convert_reduce_fusion.2
  102.9 8.5 add_convert_fusion
  111.3 6.6 copy.53
  118.0 8.9 reshape.148
  126.9 4.9 fusion.27
  131.8 11.1 %fusion.1 = (f32[2,12,512]{2,1,0:T(8,128)S(1)}, f32[2,12,512,512]{2,3,1,0:T(8,128)}) fusion(pred[2,512]{1,0:T(4,128)(4,1)S(1)} %iota_compare_fusion, bf16[2,512,1,12,64]{1,0,4,3,2:T(2,128)(2,1)S(1)} %get-tuple-element.100, bf16[2,512,1,12,64]{1,0,4,3,2:T(2,128)(2,1)S(1)} %get-tuple-element.99), kind=kOutput, calls=%fused_computation.8 | convolution fusion | flops 824168448 | bytes 28361728 | tf_op jit(solution)/shard_map/sqhc,skhc->shqk/dot_general | solution.py:41
  142.9 12.4 %fusion = f32[2,12,512]{2,1,0:T(8,128)S(1)} fusion(f32[2,12,512,512]{2,3,1,0:T(8,128)} %get-tuple-element.109, f32[2,12,512]{2,1,0:T(8,128)S(1)} %get-tuple-element.108, pred[2,512]{1,0:T(4,128)(4,1)S(1)} %iota_compare_fusion), kind=kLoop, calls=%fused_computation.6 | loop fusion | flops 25153536 | bytes 25265152 | tf_op jit(solution)/shard_map/reduce_sum | solution.py:103
  155.3 3.4 copy-done
  158.7 6.3 divide_convert_fusion
  165.1 2.0 fusion.15
  167.1 2.6 copy-done.1
  169.6 1.6 copy.58
  171.3 1.6 copy.76
  172.8 3.9 fusion.31
  177.2 48.1 %all-gather.9.cloned.1.call-done = bf16[768,3072]{1,0:T(8,128)(2,1)} async-done(((bf16[48,3072]{1,0:T(8,128)(2,1)}), bf16[768,3072]{1,0:T(8,128)(2,1)}) %all-gather.9.cloned.1.call-update) | async-done | bytes 4718608 | tf_op jit(solution)/shard_map/all_gather | solution.py:81
  225.3 12.2 %multiply_convert_fusion.1 = (bf16[1024,3072]{1,0:T(8,128)(2,1)}, f32[1024,3072]{1,0:T(8,128)}) fusion(f32[3072]{0:T(1024)S(1)} %convert_element_type.196, bf16[768,3072]{1,0:T(8,128)(2,1)} %all-gather.9.cloned.1.call-done, f32[1024,768]{1,0:T(8,128)S(1)} %get-tuple-element.111, f32[768]{0:T(1024)S(1)} %convert_element_type.193, ...), kind=kOutput, calls=%fused_computation.16 | convolution fusion | flops 4854644736 | bytes 26765312 | tf_op jit(solution)/shard_map/dot_general | solution.py:117
  237.4 69.6 %all-gather.11.cloned.1.call-done = bf16[3072,768]{1,0:T(8,128)(2,1)} async-done(((bf16[192,768]{1,0:T(8,128)(2,1)}), bf16[3072,768]{1,0:T(8,128)(2,1)}) %all-gather.11.cloned.1.call-update) | async-done | bytes 4718608 | tf_op jit(solution)/shard_map/all_gather | solution.py:83
  307.1 8.8 fusion.32
  316.4 0.9 copy-done.5
  317.3 1.3 fusion.14
  318.6 2.3 convert_reduce_fusion.3
  321.5 13.3 %convert_reduce_fusion = (f32[3072]{0:T(1024)S(1)}, bf16[1024,3072]{1,0:T(8,128)(2,1)S(1)}) fusion(f32[1024,3072]{1,0:T(8,128)} %get-tuple-element.113, f32[3072]{0:T(1024)S(1)} %convert_element_type.196, bf16[3072,768]{1,0:T(8,128)(2,1)S(1)} %copy-done.17, f32[1024,768]{1,0:T(8,128)S(1)} %get-tuple-element.93), kind=kOutput, calls=%fused_computation.15 | convolution fusion | flops 4873516032 | bytes 26763264 | tf_op jit(solution)/shard_map/rd,fd->rf/dot_general | solution.py:147
  334.8 6.0 multiply_reduce_fusion.1
  340.9 1.1 convert_reduce_fusion.4
  342.0 1.8 copy-done.13
  343.8 2.8 fusion.20
  346.6 4.8 convolution_convert_fusion.1
  351.4 2.6 copy.59
  354.0 3.8 reshape.150
  357.8 10.1 convolution_bitcast_fusion.1
  368.0 19.9 %multiply_reduce_fusion = (f32[2,12,512]{2,1,0:T(8,128)S(1)}, f32[2,12,512,512]{2,3,1,0:T(8,128)}) fusion(f32[2,12,512,512]{2,3,1,0:T(8,128)} %get-tuple-element.109, f32[2,12,512]{2,1,0:T(8,128)S(1)} %log_add_fusion, pred[2,512]{1,0:T(4,128)(4,1)S(1)} %iota_compare_fusion, bf16[2,512,1,12,64]{1,0,4,3,2:T(2,128)(2,1)} %copy-done.4, ...), kind=kOutput, calls=%fused_computation.1 | convolution fusion | flops 836751360 | bytes 53576704 | tf_op jit(solution)/shard_map/sqhc,skhc->shqk/dot_general | solution.py:189
  388.0 21.8 %multiply_convert_fusion = bf16[2,12,512,512]{2,3,1,0:T(8,128)(2,1)} fusion(f32[2,12,512,512]{2,3,1,0:T(8,128)} %get-tuple-element.118, f32[2,12,512,512]{2,3,1,0:T(8,128)} %get-tuple-element.109, f32[2,12,512]{2,1,0:T(8,128)S(1)} %get-tuple-element.117, f32[2,12,512]{2,1,0:T(8,128)S(1)} %log_add_fusion, pred[2,512]{1,0:T(4,128)(4,1)S(1)} %iota_compare_fusion), kind=kLoop, calls=%fused_computation | loop fusion | flops 37748736 | bytes 63013888 | tf_op jit(solution)/shard_map/convert_element_type | solution.py:199
  409.8 8.6 multiply_bitcast_fusion
  418.5 6.9 multiply_bitcast_fusion.1
  425.4 2.8 convert_reduce_fusion.1
  428.2 9.4 copy.65
  437.6 4.0 copy.78
  441.6 2.3 copy-done.10
  443.9 5.8 convolution_bitcast_fusion
  449.7 8.0 copy.71
  457.8 10.7 %fusion.33 = f32[768,3072]{1,0:T(8,128)} fusion(bf16[1024,3072]{1,0:T(8,128)(2,1)} %copy-done.8, f32[1024,768]{1,0:T(8,128)S(1)} %get-tuple-element.111, f32[768]{0:T(1024)S(1)} %convert_element_type.193, f32[768]{0:T(1024)S(1)} %convert_element_type.192, f32[1024]{0:T(1024)S(1)} %add_rsqrt_fusion.1, f32[1024]{0:T(1024)S(1)} %broadcast_multiply_fusion.4), kind=kOutput, calls=%fused_computation.94 | convolution fusion | flops 4835770368 | bytes 18888704 | tf_op jit(solution)/shard_map/rd,rf->df/dot_general | solution.py:152
  468.5 1.8 copy-done.12
  470.4 10.5 %fusion.23 = f32[3072,768]{1,0:T(8,128)} fusion(bf16[1024,3072]{1,0:T(8,128)(2,1)} %get-tuple-element.112, f32[1024,768]{1,0:T(8,128)S(1)} %copy-done.12), kind=kOutput, calls=%fused_computation.85 | convolution fusion | flops 4832624640 | bytes 18874368 | tf_op jit(solution)/shard_map/rf,rd->fd/dot_general | solution.py:144
  483.4 75.4 %all-reduce.16 = (bf16[1536]{0:T(1024)(128)(2,1)S(1)}, bf16[768]{0:T(1024)(128)(2,1)S(1)}, bf16[768]{0:T(1024)(128)(2,1)S(1)}, bf16[768]{0:T(1024)(128)(2,1)S(1)...) all-reduce(f32[1536]{0:T(1024)S(1)} %pad_maximum_fusion.1, ...), channel_id=3, replica_groups=mesh['dp'=2,'fsdp'=16] {'fsdp'}, use_global_device_ids=true, to_apply=%region_14.15.clone | all-reduce | flops 9216 | bytes 55296
  559.4 2.5 all-reduce.18
  566.0 1.6 convert_element_type.218
  567.6 84.3 %reduce-scatter.13.cloned.1.call-done = f32[48,2304]{1,0:T(8,128)} async-done(((f32[768,2304]{1,0:T(8,128)}), f32[48,2304]{1,0:T(8,128)}) %reduce-scatter.13.cloned.1.call-update) | async-done | bytes 442384
  651.9 2.1 copy.72
  654.0 173.6 %reduce-scatter.9.cloned.1.call-done = f32[48,3072]{1,0:T(8,128)} async-done(((f32[768,3072]{1,0:T(8,128)}), f32[48,3072]{1,0:T(8,128)}) %reduce-scatter.9.cloned.1.call-update) | async-done | bytes 589840 | tf_op jit(solution)/shard_map/reduce_scatter | solution.py:159
  827.5 1.8 convert_element_type.227
  829.3 173.7 %reduce-scatter.11.cloned.1.call-done = f32[192,768]{1,0:T(8,128)} async-done(((f32[3072,768]{1,0:T(8,128)}), f32[192,768]{1,0:T(8,128)}) %reduce-scatter.11.cloned.1.call-update) | async-done | bytes 589840 | tf_op jit(solution)/shard_map/reduce_scatter | solution.py:161
  1003.0 1.8 convert_element_type.232
  1004.9 8.5 add_convert_fusion.1
  1013.4 12.6 %all-reduce.22.cloned.1.call-done = (bf16[48,2304]{0,1:T(8,128)(2,1)}, bf16[48,768]{1,0:T(8,128)(2,1)}, bf16[48,3072]{1,0:T(8,128)(2,1)}, bf16[192,768]{1,0:T(8,128)(2,1)}) async-done(((bf16[48,2304]{0,1:T(8,128)(2,1)}, bf16[48,768]{1,0:T(8,128)(2,1)}, bf16[48,3072]{1,0:T(8,128)(2,1)}, bf16[192,768]{1,0:T(8,128)(2,1)}), (bf16[48,2304]{0,1:T(8,128)(2,1)}, bf16[48,768]{1,0:T(8,128)(2,1)}, ...) | async-done | bytes 884752 | tf_op jit(solution)/shard_map/psum | solution.py:238
  1026.0 2.0 copy.66
  1028.0 1.6 convert_element_type.219
  1029.6 1.8 convert_element_type.228
  1031.4 1.8 convert_element_type.233
  (112 shorter events, 13.7 us)
Async XLA Ops:
  7.2 95.7 %all-gather.5.cloned.1.call-start = ((), (), s32[]{:S(2)}) async-start(), calls=%async_computation.4 | async-start | bytes 3760128 | tf_op jit(solution)/shard_map/all_gather | solution.py:73
  7.9 164.9 %all-gather.7.cloned.1.call-start = ((), (), s32[]{:S(2)}) async-start(), calls=%async_computation.5 | async-start | bytes 1253376 | tf_op jit(solution)/shard_map/all_gather | solution.py:75
  8.7 216.6 %all-gather.9.cloned.1.call-start = ((), (), s32[]{:S(2)}) async-start(), calls=%async_computation.6 | async-start | bytes 5013504 | tf_op jit(solution)/shard_map/all_gather | solution.py:81
  9.4 297.7 %all-gather.11.cloned.1.call-start = ((), (), s32[]{:S(2)}) async-start(), calls=%async_computation.7 | async-start | bytes 5013504 | tf_op jit(solution)/shard_map/all_gather | solution.py:83
  10.0 556.0 %reduce-scatter.7.cloned.1.call-start = ((), (), s32[]{:S(2)}) async-start(), calls=%async_computation.8 | async-start | bytes 2506752 | tf_op jit(solution)/shard_map/reduce_scatter | solution.py:232
  131.8 11.2 %copy-start.2 = (bf16[2,512,1,12,64]{1,0,4,3,2:T(2,128)(2,1)}, bf16[2,512,1,12,64]{1,0,4,3,2:T(2,128)(2,1)S(1)}, u32[]{:S(2)}) copy-start(bf16[2,512,1,12,64]{1,0,4,3,2:T(2,128)(2,1)S(1)} %get-tuple-element.100) | copy-start | bytes 4718596
  131.8 11.1 %copy-start.6 = (bf16[2,512,1,12,64]{1,0,4,3,2:T(2,128)(2,1)}, bf16[2,512,1,12,64]{1,0,4,3,2:T(2,128)(2,1)S(1)}, u32[]{:S(2)}) copy-start(bf16[2,512,1,12,64]{1,0,4,3,2:T(2,128)(2,1)S(1)} %get-tuple-element.99) | copy-start | bytes 4718596
  131.8 33.3 %copy-start.4 = (bf16[2,512,1,12,64]{1,0,4,3,2:T(2,128)(2,1)}, bf16[2,512,1,12,64]{1,0,4,3,2:T(2,128)(2,1)S(1)}, u32[]{:S(2)}) copy-start(bf16[2,512,1,12,64]{1,0,4,3,2:T(2,128)(2,1)S(1)} %get-tuple-element.98) | copy-start | bytes 4718596
  142.9 15.8 %copy-start = (f32[2,12,512,512]{2,3,1,0:T(8,128)S(1)}, f32[2,12,512,512]{2,3,1,0:T(8,128)}, u32[]{:S(2)}) copy-start(f32[2,12,512,512]{2,3,1,0:T(8,128)} %get-tuple-element.109) | copy-start | bytes 75497472
  165.1 4.6 copy-start.1
  315.9 1.4 copy-start.5
  318.6 2.9 copy-start.17
  318.6 16.2 %slice-start = ((s8[4718592]{0:T(1024)(128)(4,1)}), s8[4194304]{0:T(1024)(128)(4,1)S(1)}, s32[]{:S(2)}) async-start(s8[4718592]{0:T(1024)(128)(4,1)} %bitcast.105), calls=%async_computation.13 | async-start | bytes 8388608
  320.9 13.9 %copy-start.11 = (f32[1024,768]{1,0:T(8,128)}, f32[1024,768]{1,0:T(8,128)S(1)}, u32[]{:S(2)}) copy-start(f32[1024,768]{1,0:T(8,128)S(1)} %get-tuple-element.93) | copy-start | bytes 9437188
  321.5 13.3 %slice-start.1 = ((s8[4718592]{0:T(1024)(128)(4,1)}), s8[524288]{0:T(1024)(128)(4,1)S(1)}, s32[]{:S(2)}) async-start(s8[4718592]{0:T(1024)(128)(4,1)} %bitcast.105), calls=%async_computation.14 | async-start | bytes 1048576
  334.8 6.1 copy-start.8
  340.9 2.9 copy-start.15
  342.0 1.8 copy-start.13
  368.0 283.9 %reduce-scatter.13.cloned.1.call-start = ((), (), s32[]{:S(2)}) async-start(), calls=%async_computation.11 | async-start | bytes 7520256
  388.0 21.8 %copy-start.7 = (bf16[2,512,1,12,64]{1,0,4,3,2:T(2,128)(2,1)S(1)}, bf16[2,512,1,12,64]{1,0,4,3,2:T(2,128)(2,1)}, u32[]{:S(2)}) copy-start(bf16[2,512,1,12,64]{1,0,4,3,2:T(2,128)(2,1)} %copy-done.6) | copy-start | bytes 4718596
  409.8 8.7 copy-start.3
  418.5 6.9 copy-start.9
  437.6 6.3 copy-start.18
  441.6 2.3 copy-start.10
  457.8 369.8 %reduce-scatter.9.cloned.1.call-start = ((), (), s32[]{:S(2)}) async-start(), calls=%async_computation.9 | async-start | bytes 10027008 | tf_op jit(solution)/shard_map/reduce_scatter | solution.py:159
  468.5 1.9 copy-start.12
  468.5 534.5 %reduce-scatter.11.cloned.1.call-start = ((), (), s32[]{:S(2)}) async-start(), calls=%async_computation.10 | async-start | bytes 10027008 | tf_op jit(solution)/shard_map/reduce_scatter | solution.py:161
  480.8 2.6 copy-start.16
  480.9 524.0 %copy-start.14 = (f32[1024,768]{1,0:T(8,128)S(1)}, f32[1024,768]{1,0:T(8,128)}, u32[]{:S(2)}) copy-start(f32[1024,768]{1,0:T(8,128)} %copy-done.13) | copy-start | bytes 9437188
  480.9 545.1 %all-reduce.22.cloned.1.call-start = ((), (), s32[]{:S(2)}) async-start(), calls=%async_computation.12 | async-start | bytes 2506752 | tf_op jit(solution)/shard_map/psum | solution.py:238
Sparse Core Ops, SparseCore 0:
  10.8 74.5 all-gather.4
  88.2 54.8 all-gather.6
  145.9 79.3 all-gather.8
  227.9 79.0 all-gather.10
  368.1 127.1 reduce-scatter.6
  501.3 150.4 reduce-scatter.12
  658.5 168.9 reduce-scatter.8
  833.2 169.7 reduce-scatter.10
  1006.9 18.9 all-reduce.21
where the time goes:
time: 1050 us; the launch traced here: 1040 us
  waiting for transfers between devices  565 us (54%)
  blocking collectives  157 us (15%)
  matrix products  154 us (15%)
  local copies, waits for them, and re-layouts  77.7 us (7%)
  other arithmetic  67.1 us (6%)
  between operations  19 us (2%)
    reduce_scatter x1, waiting for transfers between devices, shards(): lax.psum_scatter(grad_down_weight, 'fsdp', scatter_dimension=0, tiled=True)  174 us
    reduce_scatter x1, waiting for transfers between devices, shards(): lax.psum_scatter(grad_up_weight, 'fsdp', scatter_dimension=0, tiled=True)  174 us
    unnamed x2, blocking collectives  155 us
    unnamed x10, waiting for transfers between devices  87 us
    all_gather x1, waiting for transfers between devices, shards(): lax.all_gather(down_projection_weight, 'fsdp', axis=0, tiled=True)  69.6 us
    all_gather x1, waiting for transfers between devices, shards(): lax.all_gather(widening_matrix, 'fsdp', axis=0, tiled=True)  48.1 us
    unnamed x73, local copies, waits for them, and re-layouts  39.6 us
    convert_element_type x1, other arithmetic, shards(): score_grad = (softmax_again * (prob_grad - row_dot)).astype(jnp.bfloat16)  21.8 us
  transfers between devices with their start and end apart: 9, of which 6 were waited for; matrix products, arithmetic and copies ran while one was open for 21% of the time, Pallas kernels for 0%

commit v1 on v0

v1 whole, which is shorter than its diff:
```python
import functools

import jax
import jax.numpy as jnp
from jax import lax
from jax.experimental import pallas as pl
from jax.experimental.pallas import tpu as pltpu
from jax.sharding import PartitionSpec as P

HEAD_DIM = 64
GROUP = 256
HEADS = GROUP // HEAD_DIM
LANES = 128
PIECES = 16
TILE = 256
EPSILON = 1e-12
MASKED = -1e30
VMEM = 60 << 20
NN = (((1,), (0,)), ((), ()))
NT = (((1,), (1,)), ((), ()))
TN = (((0,), (0,)), ((), ()))
LOW, FULL = jnp.bfloat16, jnp.float32
ANY = pl.BlockSpec(memory_space=pl.ANY)


def dot(left, right, dims=NN):
    return lax.dot_general(left, right, dims, preferred_element_type=FULL)


def shape(dims, dtype):
    return jax.ShapeDtypeStruct(dims, dtype)


def whole(dims):
    return pl.BlockSpec(dims, lambda *at: (0,) * len(dims))


def params():
    return pltpu.CompilerParams(vmem_limit_bytes=VMEM)


def cost(flops, moved, exps=0):
    return pl.CostEstimate(flops=int(flops), bytes_accessed=int(moved), transcendentals=int(exps))


def norm_parts(values):
    centred = values - jnp.mean(values, axis=-1, keepdims=True)
    inv_root = lax.rsqrt(jnp.mean(centred * centred, axis=-1, keepdims=True) + EPSILON)
    return centred * inv_root, inv_root


def norm_back(grad_in, standard, inv_root, gain_vec):
    scaled = grad_in * gain_vec
    return inv_root * (
        scaled
        - jnp.mean(scaled, axis=-1, keepdims=True)
        - standard * jnp.mean(scaled * standard, axis=-1, keepdims=True)
    )


def column_sum(values):
    return jnp.sum(values, axis=0, keepdims=True)


def swap_cores(values):
    return lax.ppermute(values, "dp", [(0, 1), (1, 0)])


def plane_swap(values, step):
    first, second = (1, 2) if step == 0 else (2, 1)
    pairs = [(i, i ^ first) for i in range(16)] + [(16 + i, 16 + (i ^ second)) for i in range(16)]
    return lax.ppermute(values, ("dp", "fsdp"), pairs)


def z_swap(values, m):
    return lax.ppermute(values, "fsdp", [(i, i ^ (4 * m)) for i in range(16)])


def piece_of(place, core, k):
    mz, m1, m2 = k % 4, (k // 4) % 2, k // 8
    low = jnp.where(core == 0, m1 + 2 * m2, 2 * m1 + m2)
    return place ^ (4 * mz + low)


def gather_halves(piece):
    first = jnp.stack([piece] + [z_swap(piece, m) for m in (1, 2, 3)])
    second = jnp.concatenate([first, plane_swap(first, 0)])
    third = plane_swap(second, 1)
    return second, third, swap_cores(second), swap_cores(third)


def add_low(left, right):
    return (left.astype(FULL) + right.astype(FULL)).astype(LOW)


def scatter_halves(mine, theirs):
    came = swap_cores(theirs)
    sent = plane_swap(add_low(mine[8:], came[8:]), 1)
    half = mine[:8].astype(FULL) + came[:8].astype(FULL) + sent.astype(FULL)
    sent = plane_swap(half[4:].astype(LOW), 0)
    quarter = half[:4] + sent.astype(FULL)
    parts = [z_swap(quarter[m].astype(LOW), m) for m in (1, 2, 3)]
    return quarter[0] + sum(p.astype(FULL) for p in parts)


def half_of(values, which, axis=1):
    width = values.shape[axis] // 2
    return lax.dynamic_slice_in_dim(values, which * width, width, axis)


def join_halves(mine, core):
    other = swap_cores(mine)
    return jnp.where(
        core == 0, jnp.concatenate([mine, other], axis=1), jnp.concatenate([other, mine], axis=1)
    )


def copies_of(table, stacks, rows, width, skip, target, column_stride, sem):
    copies = []
    for half in range(2):
        for k in range(PIECES):
            row = pl.multiple_of(table[half, k] * rows, 16)
            column = pl.multiple_of(table[2, half] * column_stride, LANES)
            copies.append(
                pltpu.make_async_copy(
                    stacks[2 * half + k // 8].at[k % 8, :, pl.ds(skip, width)],
                    target.at[pl.ds(row, rows), pl.ds(column, width)],
                    sem,
                )
            )
    return copies


def start(copies):
    for copy in copies:
        copy.start()


def wait(copies):
    for copy in copies:
        copy.wait()


def head_mask(h, dims):
    lane = lax.broadcasted_iota(jnp.int32, dims, 1)
    return (lane >= HEAD_DIM * h) & (lane < HEAD_DIM * (h + 1))


def spread(vec, count, at):
    rows = vec.shape[0] // PIECES
    runs = [
        vec[rows * p : rows * (p + 1), at + j : at + j + 1] for p in range(PIECES) for j in range(count)
    ]
    tall = jnp.concatenate(runs, axis=0)
    return jnp.broadcast_to(tall, (tall.shape[0], LANES)).T[0:1]


def attend_kernel(
    table, lengths, tokens, s0, s1, s2, s3,
    q_out, k_out, v_out, e_out, attended, attended_full, inv_out, vectors, up_bias,
    weight, vec, bias, sem,
):
    seq, group = pl.program_id(0), pl.program_id(1)
    width = weight.shape[0]
    rows, half = width // PIECES, weight.shape[1] // 2
    stacks = (s0, s1, s2, s3)

    @pl.when((seq == 0) & (group == 0))
    def _():
        small = [
            pltpu.make_async_copy(
                stacks[k // 8].at[k % 8, :, pl.ds(half, LANES)],
                vec.at[pl.ds(pl.multiple_of(table[0, k] * rows, 16), rows)],
                sem.at[0],
            )
            for k in range(PIECES)
        ]
        large = copies_of(table, stacks, rows, half, 0, weight, half, sem.at[1])
        start(small)
        start(large)
        wait(small)
        values = vec[...].astype(FULL)
        vectors[...] = values.T[0:16]
        qv = spread(values, 2, 0)
        up_bias[...] = spread(values, 4, 8)
        bias[...] = jnp.zeros_like(bias)
        bias[:, 0:width] = qv[:, 0:width]
        bias[:, 2 * width : 3 * width] = qv[:, width : 2 * width]
        wait(large)

    rows_in = tokens[...]
    at = pl.multiple_of(group * GROUP, GROUP)

    def project(i):
        columns = pl.ds(i * width + at, GROUP)
        return (dot(rows_in, weight[:, columns]) + bias[:, columns]).astype(LOW)

    q, k, v = project(0), project(1), project(2)
    q_out[...], k_out[...], v_out[...] = q, k, v
    scaled = q * LOW(0.125)
    dims = q.shape
    keep = lax.broadcasted_iota(jnp.int32, (1, dims[0]), 1) < lengths[seq]
    total = jnp.zeros(dims, FULL)
    inv = jnp.zeros(dims, FULL)
    for h in range(HEADS):
        mask = head_mask(h, dims)
        scores = jnp.where(keep, dot(scaled, jnp.where(mask, k, LOW(0)), NT), MASKED)
        exps = jnp.exp(scores - jnp.max(scores, axis=1, keepdims=True))
        row_total = jnp.sum(exps, axis=1, keepdims=True)
        low = exps.astype(LOW)
        e_out[h] = low
        total = total + dot(low, jnp.where(mask, v, LOW(0)))
        inv = jnp.where(mask, 1.0 / row_total, inv)
    result = total * inv
    inv_out[...] = inv
    attended_full[...] = result
    attended[...] = result.astype(LOW)


def attend(table, lengths, tokens, stacks):
    seqs, length, width = tokens.shape
    groups = width // GROUP
    rows = seqs * length
    block = pl.BlockSpec((length, GROUP), lambda s, g, *_: (s, g))
    heads = width // HEAD_DIM
    return pl.pallas_call(
        attend_kernel,
        grid_spec=pltpu.PrefetchScalarGridSpec(
            num_scalar_prefetch=2,
            grid=(seqs, groups),
            in_specs=[pl.BlockSpec((length, width), lambda s, g, *_: (s, 0))] + [ANY] * 4,
            out_specs=[block] * 3
            + [pl.BlockSpec((HEADS, length, length), lambda s, g, *_: (s * groups + g, 0, 0))]
            + [block] * 3
            + [whole((16, width)), whole((1, 4 * width))],
            scratch_shapes=[
                pltpu.VMEM((width, 3 * width), LOW),
                pltpu.VMEM((width, LANES), LOW),
                pltpu.VMEM((1, 3 * width), FULL),
                pltpu.SemaphoreType.DMA((2,)),
            ],
        ),
        out_shape=[shape((rows, width), LOW)] * 3
        + [
            shape((seqs * heads, length, length), LOW),
            shape((rows, width), LOW),
            shape((rows, width), FULL),
            shape((rows, width), FULL),
            shape((16, width), FULL),
            shape((1, 4 * width), FULL),
        ],
        compiler_params=params(),
        cost_estimate=cost(16e9, 30e6),
        name="attend",
    )(table, lengths, tokens.reshape(rows, width), *stacks)


def widen_kernel(
    table, attended, tokens, vectors, up_bias, s0, s1, s2, s3,
    normed, standard, root, active, slope,
    out_weight, up_weight, sem,
):
    width = out_weight.shape[0]
    rows, half = width // PIECES, width // 2
    stacks = (s0, s1, s2, s3)
    first = pl.program_id(0) == 0
    small = copies_of(table, stacks, rows, half, 0, out_weight, half, sem.at[0])
    large = copies_of(table, stacks, rows, 4 * half, half, up_weight, 4 * half, sem.at[1])

    @pl.when(first)
    def _():
        start(small)
        start(large)
        wait(small)

    values = tokens[...].astype(FULL) + dot(attended[...], out_weight[...]) + vectors[2:3]
    n, s = norm_parts(values)
    standard[...] = n
    root[...] = jnp.broadcast_to(s, root.shape)
    low = (n * vectors[3:4] + vectors[4:5]).astype(LOW)
    normed[...] = low

    @pl.when(first)
    def _():
        wait(large)

    for c in range(4):
        columns = slice(c * width, (c + 1) * width)
        hidden = dot(low, up_weight[:, columns]) + up_bias[:, columns]
        part = 0.5 * (1.0 + lax.erf(hidden * 0.7071067811865476))
        density = jnp.exp(-0.5 * hidden * hidden) * 0.3989422804014327
        active[:, columns] = (hidden * part).astype(LOW)
        slope[:, columns] = (part + hidden * density).astype(LOW)


def widen(table, attended, tokens, vectors, up_bias, stacks):
    rows, width = attended.shape
    row = lambda w: pl.BlockSpec((TILE, w), lambda i, *_: (i, 0))
    return pl.pallas_call(
        widen_kernel,
        grid_spec=pltpu.PrefetchScalarGridSpec(
            num_scalar_prefetch=1,
            grid=(rows // TILE,),
            in_specs=[row(width), row(width), whole(vectors.shape), whole(up_bias.shape)] + [ANY] * 4,
            out_specs=[row(width), row(width), row(LANES), row(4 * width), row(4 * width)],
            scratch_shapes=[
                pltpu.VMEM((width, width), LOW),
                pltpu.VMEM((width, 4 * width), LOW),
                pltpu.SemaphoreType.DMA((2,)),
            ],
        ),
        out_shape=[
            shape((rows, width), LOW),
            shape((rows, width), FULL),
            shape((rows, LANES), FULL),
            shape((rows, 4 * width), LOW),
            shape((rows, 4 * width), LOW),
        ],
        compiler_params=params(),
        cost_estimate=cost(12e9, 30e6),
        name="widen",
    )(table, attended, tokens.reshape(rows, width), vectors, up_bias, *stacks)


def narrow_kernel(
    table, active, slope, normed, standard, root, cotangent, vectors, u0, u1, u2, u3, d0, d1, d2, d3,
    output, branch_two, pre_grad, branch_one, attended_grad, sums, up_sum,
    out_weight, up_weight, down_weight, sem,
):
    width = out_weight.shape[0]
    rows, half = width // PIECES, width // 2
    first = pl.program_id(0) == 0
    ups, downs = (u0, u1, u2, u3), (d0, d1, d2, d3)
    out_copies = copies_of(table, ups, rows, half, 0, out_weight, half, sem.at[0])
    up_copies = copies_of(table, ups, rows, 4 * half, half, up_weight, 4 * half, sem.at[1])
    down_copies = copies_of(table, downs, 4 * rows, half, 0, down_weight, half, sem.at[2])

    @pl.when(first)
    def _():
        start(down_copies)
        start(up_copies)
        start(out_copies)
        sums[...] = jnp.zeros_like(sums)
        up_sum[...] = jnp.zeros_like(up_sum)
        wait(down_copies)

    values = normed[...].astype(FULL) + dot(active[...], down_weight[...]) + vectors[5:6]
    n2, s2 = norm_parts(values)
    output[...] = (n2 * vectors[6:7] + vectors[7:8]).astype(LOW)
    grad = cotangent[...].astype(FULL)
    second = norm_back(grad, n2, s2, vectors[6:7])
    low = second.astype(LOW)
    branch_two[...] = low
    sums[0:1] += column_sum(grad * n2)
    sums[1:2] += column_sum(grad)
    sums[2:3] += column_sum(low.astype(FULL))

    @pl.when(first)
    def _():
        wait(up_copies)

    normed_grad = second
    for c in range(4):
        columns = slice(c * width, (c + 1) * width)
        part = (dot(low, down_weight[columns], NT) * slope[:, columns].astype(FULL)).astype(LOW)
        pre_grad[:, columns] = part
        up_sum[:, columns] += column_sum(part.astype(FULL))
        normed_grad = normed_grad + dot(part, up_weight[:, columns], NT)
    n1 = standard[...]
    sums[3:4] += column_sum(normed_grad * n1)
    sums[4:5] += column_sum(normed_grad)
    low = norm_back(normed_grad, n1, root[:, 0:1], vectors[3:4]).astype(LOW)
    branch_one[...] = low
    sums[5:6] += column_sum(low.astype(FULL))

    @pl.when(first)
    def _():
        wait(out_copies)

    attended_grad[...] = dot(low, out_weight[...], NT).astype(LOW)


def narrow(table, active, slope, normed, standard, root, cotangent, vectors, ups, downs):
    rows, width = normed.shape
    row = lambda w: pl.BlockSpec((TILE, w), lambda i, *_: (i, 0))
    return pl.pallas_call(
        narrow_kernel,
        grid_spec=pltpu.PrefetchScalarGridSpec(
            num_scalar_prefetch=1,
            grid=(rows // TILE,),
            in_specs=[row(4 * width), row(4 * width), row(width), row(width), row(LANES), row(width)]
            + [whole(vectors.shape)]
            + [ANY] * 8,
            out_specs=[row(width), row(width), row(4 * width), row(width), row(width)]
            + [whole((8, width)), whole((1, 4 * width))],
            scratch_shapes=[
                pltpu.VMEM((width, width), LOW),
                pltpu.VMEM((width, 4 * width), LOW),
                pltpu.VMEM((4 * width, width), LOW),
                pltpu.SemaphoreType.DMA((3,)),
            ],
        ),
        out_shape=[
            shape((rows, width), LOW),
            shape((rows, width), LOW),
            shape((rows, 4 * width), LOW),
            shape((rows, width), LOW),
            shape((rows, width), LOW),
            shape((8, width), FULL),
            shape((1, 4 * width), FULL),
        ],
        compiler_params=params(),
        cost_estimate=cost(24e9, 40e6),
        name="narrow",
    )(table, active, slope, normed, standard, root, cotangent.reshape(rows, width), vectors, *ups, *downs)


def down_grad_kernel(order, active, branch_two, mine, theirs):
    step = pl.program_id(0)
    width = branch_two.shape[1]
    rows, half = 4 * width // PIECES, width // 2
    result = dot(active[...], branch_two[...], TN).astype(LOW)
    for p in range(4):
        block = result[rows * p : rows * (p + 1)]
        core = order[2, 0]

        @pl.when(core == 0)
        def _():
            mine[order[0, 4 * step + p]] = block[:, :half]
            theirs[order[1, 4 * step + p]] = block[:, half:]

        @pl.when(core == 1)
        def _():
            mine[order[0, 4 * step + p]] = block[:, half:]
            theirs[order[1, 4 * step + p]] = block[:, :half]


def down_grad(order, active, branch_two):
    rows, width = branch_two.shape
    stack = (PIECES, 4 * width // PIECES, width // 2)
    return pl.pallas_call(
        down_grad_kernel,
        grid_spec=pltpu.PrefetchScalarGridSpec(
            num_scalar_prefetch=1,
            grid=(4,),
            in_specs=[pl.BlockSpec((rows, width), lambda i, *_: (0, i)), whole((rows, width))],
            out_specs=[whole(stack)] * 2,
        ),
        out_shape=[shape(stack, LOW)] * 2,
        compiler_params=params(),
        cost_estimate=cost(7e9, 14e6),
        name="down_grad",
    )(order, active, branch_two)


def put_pieces(order, result, mine, theirs, to_mine, at):
    rows = result.shape[0] // PIECES
    width = result.shape[1]
    for p in range(PIECES):
        block = result[rows * p : rows * (p + 1)]

        @pl.when(to_mine)
        def _():
            mine[order[0, p], :, at : at + width] = block

        @pl.when(jnp.logical_not(to_mine))
        def _():
            theirs[order[1, p], :, at : at + width] = block


def up_grad_kernel(order, normed, pre_grad, attended, branch_one, mine, theirs):
    step = pl.program_id(0)
    width = normed.shape[1]
    half = width // 2
    core = order[2, 0]

    @pl.when(step < 4)
    def _():
        result = dot(normed[...], pre_grad[...], TN).astype(LOW)
        for part in range(2):

            @pl.when(step % 2 == part)
            def _():
                put_pieces(order, result, mine, theirs, step // 2 == core, half + part * width)

    @pl.when(step == 4)
    def _():
        result = dot(attended[...], branch_one[...], TN).astype(LOW)
        for c in range(2):
            put_pieces(order, result[:, c * half : (c + 1) * half], mine, theirs, core == c, 0)


def up_grad(order, normed, pre_grad, attended, branch_one):
    rows, width = normed.shape
    stack = (PIECES, width // PIECES, 5 * width // 2)
    return pl.pallas_call(
        up_grad_kernel,
        grid_spec=pltpu.PrefetchScalarGridSpec(
            num_scalar_prefetch=1,
            grid=(5,),
            in_specs=[
                whole((rows, width)),
                pl.BlockSpec((rows, width), lambda i, *_: (0, jnp.minimum(i, 3))),
                whole((rows, width)),
                whole((rows, width)),
            ],
            out_specs=[whole(stack)] * 2,
        ),
        out_shape=[shape(stack, LOW)] * 2,
        compiler_params=params(),
        cost_estimate=cost(9e9, 18e6),
        name="up_grad",
    )(order, normed, pre_grad, attended, branch_one)


def attend_back_kernel(
    q_in, k_in, v_in, e_in, attended_full, inv_in, grad_in, q_grad, k_grad, v_grad, sums
):
    seq = pl.program_id(1)
    q, k, v = q_in[...] * LOW(0.125), k_in[...], v_in[...]
    dims = q.shape
    grad = (grad_in[...].astype(FULL) * inv_in[...]).astype(LOW)
    along = grad.astype(FULL) * attended_full[...]
    q_total, k_total, v_total = (jnp.zeros(dims, FULL) for _ in range(3))
    for h in range(HEADS):
        mask = head_mask(h, dims)
        masked = lambda values: jnp.where(mask, values, LOW(0))
        exps = e_in[h]
        shift = jnp.sum(jnp.where(mask, along, 0.0), axis=1, keepdims=True)
        score = (exps.astype(FULL) * (dot(grad, masked(v), NT) - shift)).astype(LOW)
        q_total = q_total + dot(score, masked(k))
        k_total = k_total + dot(score, masked(q), TN)
        v_total = v_total + dot(exps, masked(grad), TN)
    q_low, k_low, v_low = (q_total * 0.125).astype(LOW), k_total.astype(LOW), v_total.astype(LOW)
    q_grad[...], k_grad[...], v_grad[...] = q_low, k_low, v_low
    both = jnp.concatenate([column_sum(q_low.astype(FULL)), column_sum(v_low.astype(FULL))], axis=0)

    @pl.when(seq == 0)
    def _():
        sums[0:2] = both

    @pl.when(seq != 0)
    def _():
        sums[0:2] += both


def attend_back(q, k, v, exps, attended_full, inv, grad, length):
    rows, width = q.shape
    seqs, groups = rows // length, width // GROUP
    block = pl.BlockSpec((length, GROUP), lambda g, s: (s, g))
    return pl.pallas_call(
        attend_back_kernel,
        grid=(groups, seqs),
        in_specs=[block] * 3
        + [pl.BlockSpec((HEADS, length, length), lambda g, s: (s * groups + g, 0, 0))]
        + [block] * 3,
        out_specs=[block] * 3 + [pl.BlockSpec((8, GROUP), lambda g, s: (0, g))],
        out_shape=[shape((rows, width), LOW)] * 3 + [shape((8, width), FULL)],
        compiler_params=params(),
        cost_estimate=cost(16e9, 25e6),
        name="attend_back",
    )(q, k, v, exps, attended_full, inv, grad)


def qkv_grad_kernel(order, tokens, q_grad, k_grad, v_grad, sums, qv_sums, up_sum, mine, theirs):
    step = pl.program_id(0)
    width = tokens.shape[1]
    half = width // 2
    core = order[2, 0]
    for i, grads in enumerate((q_grad, k_grad, v_grad)):

        @pl.when(step // 2 == i)
        def _():
            result = dot(tokens[...], grads[...], TN).astype(LOW)
            for part in range(3):

                @pl.when(step % 3 == part)
                def _():
                    put_pieces(order, result, mine, theirs, step // 3 == core, part * half)

    @pl.when(step == 0)
    def _():
        rows = width // PIECES
        ones = jnp.concatenate([sums[...], qv_sums[...], jnp.zeros((LANES - 16, width), FULL)], axis=0).T
        lane = lax.broadcasted_iota(jnp.int32, (rows, LANES), 1)

        def tall(row):
            return jnp.broadcast_to(row, (LANES, row.shape[1])).T

        qv = [tall(qv_sums[i : i + 1]) for i in range(2)]
        up = [tall(up_sum[:, i * width : (i + 1) * width]) for i in range(4)]
        for p in range(PIECES):
            block = ones[rows * p : rows * (p + 1)]
            block = jnp.where(lane < 8, block, 0.0)
            for j in range(2):
                run = 2 * p + j
                at = rows * (run % PIECES)
                block = jnp.where(lane == 8 + j, qv[run // PIECES][at : at + rows], block)
            for j in range(4):
                run = 4 * p + j
                at = rows * (run % PIECES)
                block = jnp.where(lane == 10 + j, up[run // PIECES][at : at + rows], block)
            low = block.astype(LOW)
            mine[order[0, p], :, 3 * half :] = low
            theirs[order[1, p], :, 3 * half :] = low


def qkv_grad(order, tokens, q_grad, k_grad, v_grad, sums, qv_sums, up_sum):
    rows, width = q_grad.shape
    half = width // 2
    stack = (PIECES, width // PIECES, 3 * half + LANES)

    def column(i):
        return pl.BlockSpec((rows, half), lambda s, *_: (0, jnp.clip(s - 2 * i, 0, 1)))

    return pl.pallas_call(
        qkv_grad_kernel,
        grid_spec=pltpu.PrefetchScalarGridSpec(
            num_scalar_prefetch=1,
            grid=(6,),
            in_specs=[whole((rows, width)), column(0), column(1), column(2)]
            + [whole(sums.shape), whole(qv_sums.shape), whole(up_sum.shape)],
            out_specs=[whole(stack)] * 2,
        ),
        out_shape=[shape(stack, LOW)] * 2,
        compiler_params=params(),
        cost_estimate=cost(6e9, 14e6),
        name="qkv_grad",
    )(order, tokens.reshape(rows, width), q_grad, k_grad, v_grad, sums, qv_sums, up_sum)


def token_grad_kernel(table, q_grad, k_grad, v_grad, first, s0, s1, s2, s3, out, weight, sem):
    width = weight.shape[0]
    rows, half = width // PIECES, weight.shape[1] // 2
    copies = copies_of(table, (s0, s1, s2, s3), rows, half, 0, weight, half, sem)

    @pl.when(pl.program_id(0) == 0)
    def _():
        start(copies)
        wait(copies)

    total = first[...].astype(FULL)
    for i, grads in enumerate((q_grad, k_grad, v_grad)):
        total = total + dot(grads[...], weight[:, i * width : (i + 1) * width], NT)
    out[...] = total.astype(LOW)


def token_grad(table, q_grad, k_grad, v_grad, first, stacks):
    rows, width = q_grad.shape
    row = pl.BlockSpec((TILE, width), lambda i, *_: (i, 0))
    return pl.pallas_call(
        token_grad_kernel,
        grid_spec=pltpu.PrefetchScalarGridSpec(
            num_scalar_prefetch=1,
            grid=(rows // TILE,),
            in_specs=[row] * 4 + [ANY] * 4,
            out_specs=row,
            scratch_shapes=[pltpu.VMEM((width, 3 * width), LOW), pltpu.SemaphoreType.DMA],
        ),
        out_shape=shape((rows, width), LOW),
        compiler_params=params(),
        cost_estimate=cost(6e9, 12e6),
        name="token_grad",
    )(table, q_grad, k_grad, v_grad, first, *stacks)


def pack(vectors, rows):
    columns = jnp.concatenate([v.reshape(-1, rows) for v in vectors], axis=0).T
    return jnp.pad(columns, ((0, 0), (0, LANES - columns.shape[1])))


def pack_all(chips, rows, qv, out_bias, gain_one, shift_one, up_bias, down_bias, gain_two, shift_two):
    parts = (qv, out_bias, gain_one, shift_one, down_bias, gain_two, shift_two, up_bias)
    if chips == 1:
        return pack(parts, rows)
    return jnp.concatenate(
        [pack([v.reshape(chips, -1)[p] for v in parts], rows) for p in range(chips)], axis=0
    )


def shards(
    chips,
    tokens,
    lengths,
    query_key_value_weight,
    qv_bias,
    output_projection_weight,
    output_projection_bias,
    gain_one,
    shift_one,
    widening_matrix,
    widening_offset_vector,
    down_projection_weight,
    down_projection_bias,
    gain_two,
    shift_two,
    cotangent,
):
    seq_count, seq_length, width = tokens.shape
    core, place = lax.axis_index("dp"), lax.axis_index("fsdp")
    rows = query_key_value_weight.shape[0]
    small = (
        qv_bias,
        output_projection_bias,
        gain_one,
        shift_one,
        widening_offset_vector,
        down_projection_bias,
        gain_two,
        shift_two,
    )
    direct = chips == PIECES
    numbers = range(PIECES)
    if direct:
        qkv_set = gather_halves(
            jnp.concatenate([half_of(query_key_value_weight, core), pack_all(1, rows, *small)], axis=1)
        )
        up_set = gather_halves(
            jnp.concatenate([half_of(output_projection_weight, core), half_of(widening_matrix, core)], axis=1)
        )
        down_set = gather_halves(half_of(down_projection_weight, core))
        owners = [jnp.stack([piece_of(place, c, k) for k in numbers]) for c in (core, 1 - core)]
    else:
        gather = lambda values: lax.all_gather(values, "fsdp", axis=0, tiled=True)
        packed = pack_all(PIECES, width // PIECES, *(gather(v) for v in small))

        def stacks_of(make):
            both = [make(c) for c in (core, 1 - core)]
            both = [values.reshape(2, 8, -1, values.shape[1]) for values in both]
            return both[0][0], both[0][1], both[1][0], both[1][1]

        full_qkv, full_out = gather(query_key_value_weight), gather(output_projection_weight)
        full_up, full_down = gather(widening_matrix), gather(down_projection_weight)
        qkv_set = stacks_of(lambda c: jnp.concatenate([half_of(full_qkv, c), packed], axis=1))
        up_set = stacks_of(lambda c: jnp.concatenate([half_of(full_out, c), half_of(full_up, c)], axis=1))
        down_set = stacks_of(lambda c: half_of(full_down, c))
        owners = [jnp.arange(PIECES), jnp.arange(PIECES)]
    cores = jnp.stack([core, 1 - core] + [core] * 14)
    table = jnp.stack(owners + [cores]).astype(jnp.int32)
    order = jnp.stack([jnp.argsort(o) for o in owners] + [cores]).astype(jnp.int32)

    q, k, v, exps, attended, attended_full, inv, vectors, up_bias = attend(table, lengths, tokens, qkv_set)
    normed, standard, root, active, slope = widen(table, attended, tokens, vectors, up_bias, up_set)
    output, branch_two, pre_grad, branch_one, attended_grad, sums, up_sum = narrow(
        table, active, slope, normed, standard, root, cotangent, vectors, up_set, down_set
    )
    down_pair = down_grad(order, active, branch_two)
    up_pair = up_grad(order, normed, pre_grad, attended, branch_one)
    q_grad, k_grad, v_grad, qv_sums = attend_back(
        q, k, v, exps, attended_full, inv, attended_grad, seq_length
    )
    qkv_pair = qkv_grad(order, tokens, q_grad, k_grad, v_grad, sums, qv_sums, up_sum)
    grad_tokens = token_grad(table, q_grad, k_grad, v_grad, branch_one, qkv_set)

    half = width // 2
    if direct:
        down_sum, up_total, qkv_sum = (scatter_halves(*pair) for pair in (down_pair, up_pair, qkv_pair))
        vec = qkv_sum[:, 3 * half :]
        qkv_sum = qkv_sum[:, : 3 * half]
        vec_columns = lambda at, count: vec[:, at : at + count].T.reshape(-1)
    else:

        def reduce(values):
            return lax.psum_scatter(values, "fsdp", scatter_dimension=0, tiled=True)

        def totals(pair):
            both = pair[0].astype(FULL) + swap_cores(pair[1]).astype(FULL)
            return both.reshape(-1, both.shape[2])

        down_sum, up_total = reduce(totals(down_pair)), reduce(totals(up_pair))
        whole_qkv = totals(qkv_pair)
        qkv_sum = reduce(whole_qkv[:, : 3 * half])
        vec = whole_qkv[:, 3 * half :].reshape(PIECES, -1, LANES)
        vec_columns = lambda at, count: reduce(vec[:, :, at : at + count].transpose(0, 2, 1).reshape(-1))
    out_sum, up_total = up_total[:, :half], up_total[:, half:]
    return (
        output.reshape(tokens.shape),
        grad_tokens.reshape(tokens.shape),
        join_halves(qkv_sum, core),
        vec_columns(8, 2),
        join_halves(out_sum, core),
        vec_columns(5, 1),
        vec_columns(3, 1),
        vec_columns(4, 1),
        join_halves(up_total, core),
        vec_columns(10, 4),
        join_halves(down_sum, core),
        vec_columns(2, 1),
        vec_columns(0, 1),
        vec_columns(1, 1),
    )


def solution(mesh):
    tokens, lengths = P(("dp", "fsdp"), None, None), P(("dp", "fsdp"))
    matrix, vector = P("fsdp", None), P("fsdp")
    return jax.shard_map(
        functools.partial(shards, mesh.shape["fsdp"]),
        mesh=mesh,
        in_specs=(
            tokens, lengths, matrix, vector, matrix, vector, vector, vector,
            matrix, vector, matrix, vector, vector, vector, tokens,
        ),
        out_specs=(
            tokens, tokens, matrix, vector, matrix, vector, vector, vector,
            matrix, vector, matrix, vector, vector, vector,
        ),
        check_vma=False,
    )
```

time: 1050 us -> 351 us (0.33)
  waiting for transfers between devices: 565 us -> 116 us
  blocking collectives: 157 us -> 0 us
  matrix products: 154 us -> 0 us
  Pallas kernels: 0 us -> 144 us
  local copies, waits for them, and re-layouts: 77.7 us -> 16.7 us
  starting transfers between devices: 0.36 us -> 53.2 us
  other arithmetic: 67.1 us -> 19.9 us
  between operations: 19 us -> 1.11 us
    reduce_scatter x3 -> x0, waiting for transfers between devices: 347 us -> none  [the longest x1 174 us: shards(): lax.psum_scatter(grad_down_weight, 'fsdp', scatter_dimension=0, tiled=True)]
    unnamed x2 -> x0, blocking collectives: 155 us -> none
    dot_general x18 -> x0, matrix products: 154 us -> none  [the longest x1 19.9 us: shards(): jnp.einsum('sqhc,skhc->shqk', attended_grad, residual_mixed[:, :, 2], pre...]
    pallas_call x0 -> x8, Pallas kernels: none -> 144 us  [the longest x1 33.1 us: narrow(): pl.pallas_call(narrow_kernel, grid_spec=pltpu.PrefetchScalarGridSpec(num_...]
    all_gather x4 -> x0, waiting for transfers between devices: 118 us -> none  [the longest x1 69.6 us: shards(): lax.all_gather(down_projection_weight, 'fsdp', axis=0, tiled=True)]
    ppermute x0 -> x43, waiting for transfers between devices: none -> 116 us  [the longest x12 77.8 us: plane_swap(): return lax.ppermute(values, ('dp', 'fsdp'), pairs)]
    unnamed x10 -> x0, waiting for transfers between devices: 87 us -> none
    ppermute x0 -> x43, starting transfers between devices: none -> 53.2 us  [the longest x18 34.4 us: z_swap(): return lax.ppermute(values, 'fsdp', [(i, i ^ 4 * m) for i in range(16)])]
  transfers between devices with their start and end apart: 9 -> 43, of which waited for: 6 -> 15; matrix products, arithmetic and copies ran while one was open for 21% -> 9% of each run, Pallas kernels for 0% -> 22%
where the time goes in v1:
time: 351 us
  Pallas kernels  144 us (41%)
  waiting for transfers between devices  116 us (33%)
  starting transfers between devices  53.2 us (15%)
  other arithmetic  19.9 us (6%)
  local copies, waits for them, and re-layouts  16.7 us (5%)
    ppermute x12, waiting for transfers between devices, plane_swap(): return lax.ppermute(values, ('dp', 'fsdp'), pairs)  77.8 us
    ppermute x18, waiting for transfers between devices, z_swap(): return lax.ppermute(values, 'fsdp', [(i, i ^ 4 * m) for i in range(16)])  37.7 us
    ppermute x18, starting transfers between devices, z_swap(): return lax.ppermute(values, 'fsdp', [(i, i ^ 4 * m) for i in range(16)])  34.4 us
    pallas_call x1, Pallas kernels, narrow(): pl.pallas_call(narrow_kernel, grid_spec=pltpu.PrefetchScalarGridSpec(num_...  33.1 us
    pallas_call x1, Pallas kernels, attend(): pl.pallas_call(attend_kernel, grid_spec=pltpu.PrefetchScalarGridSpec(num_...  22.6 us
    pallas_call x1, Pallas kernels, attend_back(): pl.pallas_call(attend_back_kernel, grid=(groups, seqs), in_specs=[block]...  20.6 us
    pallas_call x1, Pallas kernels, widen(): pl.pallas_call(widen_kernel, grid_spec=pltpu.PrefetchScalarGridSpec(num_s...  19.1 us
    ppermute x12, starting transfers between devices, plane_swap(): return lax.ppermute(values, ('dp', 'fsdp'), pairs)  16.1 us
  transfers between devices with their start and end apart: 43, of which 15 were waited for; matrix products, arithmetic and copies ran while one was open for 9% of the time, Pallas kernels for 22%

profile of v1, /device:TPU:0, one launch (start us, length us, event | category | flops | bytes accessed | tf_op | source)
XLA Modules:
  0.0 350.6 jit_solution(970078869844710627)
XLA Ops:
  0.7 0.8 reshape.82
  1.5 0.7 reshape.89
  2.2 0.8 concatenate.45
  3.1 0.9 constant_dynamic-slice_fusion.3
  4.0 4.1 %collective-permute-start.1 = (bf16[48,1280]{1,0:T(8,128)(2,1)S(1)}, bf16[48,1280]{1,0:T(8,128)(2,1)S(1)}, u32[]{:S(2)}, u32[]{:S(2)}) collective-permute-start(bf16[48,1280]{1,0:T(8,128)(2,1)S(1)} %get-tuple-element.106), channel_id=1, source_target_pairs={{0,8},{1,9},{2,10},{3,11},{4,12},{5,13},{6,14},{7,15},{8,0},{9,1},... | collective-permute-start | bytes 368648 | tf_op jit(solution)/shard_map/ppermute | solution.py:76
  8.1 1.6 collective-permute-start
  9.7 0.8 constant_dynamic-slice_fusion.2
  10.6 2.0 collective-permute-start.8
  12.5 2.5 collective-permute-start.7
  17.1 2.0 collective-permute-start.15
  19.8 4.9 %collective-permute-start.14 = (bf16[192,384]{1,0:T(8,128)(2,1)S(1)}, bf16[192,384]{1,0:T(8,128)(2,1)S(1)}, u32[]{:S(2)}, u32[]{:S(2)}) collective-permute-start(bf16[192,384]{1,0:T(8,128)(2,1)S(1)} %get-tuple-element.93), channel_id=1, source_target_pairs={{0,4},{1,5},{2,6},{3,7},{4,0},{5,1},{6,2},{7,3},{8,12},{9,13},{10,... | collective-permute-start | bytes 442376 | tf_op jit(solution)/shard_map/ppermute | solution.py:76
  25.4 4.6 %collective-permute-done.16 = bf16[192,384]{1,0:T(8,128)(2,1)S(1)} collective-permute-done((bf16[192,384]{1,0:T(8,128)(2,1)S(1)}, bf16[192,384]{1,0:T(8,128)(2,1)S(1)}, u32[]{:S(2)}, u32[]{:S(2)}) %collective-permute-start.16) | collective-permute-done | bytes 147488 | tf_op jit(solution)/shard_map/ppermute | solution.py:76
  30.0 2.6 collective-permute-start.9
  32.6 11.3 %collective-permute-done.15 = bf16[192,384]{1,0:T(8,128)(2,1)S(1)} collective-permute-done((bf16[192,384]{1,0:T(8,128)(2,1)S(1)}, bf16[192,384]{1,0:T(8,128)(2,1)S(1)}, u32[]{:S(2)}, u32[]{:S(2)}) %collective-permute-start.15) | collective-permute-done | bytes 147488 | tf_op jit(solution)/shard_map/ppermute | solution.py:76
  43.9 1.5 collective-permute-start.3
  47.6 1.6 collective-permute-start.10
  49.2 3.5 %collective-permute-done.3 = bf16[4,48,1280]{2,1,0:T(8,128)(2,1)S(1)} collective-permute-done((bf16[4,48,1280]{2,1,0:T(8,128)(2,1)S(1)}, bf16[4,48,1280]{2,1,0:T(8,128)(2,1)S(1)}, u32[]{:S(2)}, u32[]{:S(2)}) %collective-permute-start.3) | collective-permute-done | bytes 491552 | tf_op jit(solution)/shard_map/ppermute | solution.py:72
  52.7 0.8 constant_dynamic-update-slice_fusion.s0
  53.6 1.6 collective-permute-start.4
  55.2 23.7 %collective-permute-done.10 = bf16[4,48,1920]{2,1,0:T(8,128)(2,1)S(1)} collective-permute-done((bf16[4,48,1920]{2,1,0:T(8,128)(2,1)S(1)}, bf16[4,48,1920]{2,1,0:T(8,128)(2,1)S(1)}, u32[]{:S(2)}, u32[]{:S(2)}) %collective-permute-start.10) | collective-permute-done | bytes 737312 | tf_op jit(solution)/shard_map/ppermute | solution.py:72
  78.9 2.1 collective-permute-start.11
  81.7 0.9 constant_dynamic-update-slice_fusion.10.d0
  83.5 1.2 sort.31
  84.8 1.2 sort.32
  87.2 24.0 %collective-permute-done.18.d1 = bf16[8,192,384]{2,1,0:T(8,128)(2,1)} collective-permute-done((bf16[8,192,384]{2,1,0:T(8,128)(2,1)}, bf16[8,192,384]{2,1,0:T(8,128)(2,1)}, u32[]{:S(2)}, u32[]{:S(2)}) %collective-permute-start.18) | collective-permute-done | bytes 1179680 | tf_op jit(solution)/shard_map/ppermute | solution.py:72
  111.7 22.6 %attend.1 = (bf16[1024,768]{1,0:T(8,128)(2,1)}, bf16[1024,768]{1,0:T(8,128)(2,1)}, bf16[1024,768]{1,0:T(8,128)(2,1)}, bf16[24,512,512]{2,1,0:T(8,128)(2,1)}, bf1...) custom-call(s32[3,16]{1,0:T(4,128)} %get-tuple-element.108.table, ...), custom_call_target="tpu_custom_call" | custom-call | flops 16000000000 | bytes 30000000 | tf_op jit(solution)/shard_map/attend/pallas_call | solution.py:226
  134.3 19.1 %widen.1 = (bf16[1024,768]{1,0:T(8,128)(2,1)}, f32[1024,768]{1,0:T(8,128)}, f32[1024,128]{1,0:T(8,128)}, bf16[1024,3072]{1,0:T(8,128)(2,1)}, bf16[1024,3072]{1,0:T(8,128)(2,1)}) custom-call(s32[3,16]{1,0:T(4,128)} %get-tuple-element.108.table, bf16[1024,768]{1,0:T(8,128)(2,1)} %get-tuple-element.47.attended, bf16[1024,768]{1,0:T(8,128)(2,1)} %bitcast.127, ...), custom_call_target="tpu_custom_call" | custom-call | flops 12000000000 | bytes 30000000 | tf_op jit(solution)/shard_map/widen/pallas_call | solution.py:299
  153.4 33.1 %narrow.1 = (bf16[1024,768]{1,0:T(8,128)(2,1)}, bf16[1024,768]{1,0:T(8,128)(2,1)}, bf16[1024,3072]{1,0:T(8,128)(2,1)}, bf16[1024,768]{1,0:T(8,128)(2,1)}, bf16[1...) custom-call(s32[3,16]{1,0:T(4,128)} %get-tuple-element.108.table, ...), custom_call_target="tpu_custom_call" | custom-call | flops 24000000000 | bytes 40000000 | tf_op jit(solution)/shard_map/narrow/pallas_call | solution.py:386
  186.5 20.6 %attend_back.1 = (bf16[1024,768]{1,0:T(8,128)(2,1)}, bf16[1024,768]{1,0:T(8,128)(2,1)}, bf16[1024,768]{1,0:T(8,128)(2,1)}, f32[8,768]{1,0:T(8,128)}) custom-call(bf16[1024,768]{1,0:T(8,128)(2,1)} %get-tuple-element.56.q_in, bf16[1024,768]{1,0:T(8,128)(2,1)} %get-tuple-element.57.k_in, bf16[1024,768]{1,0:T(8,128)(2,1)} %get-tuple-element.58.v_in, ...), custom_call_target="tpu_custom_call" | custom-call | flops 16000000000 | bytes 25000000 | tf_op jit(solution)/shard_map/attend_back/pallas_call | solution.py:551
  207.1 12.9 %qkv_grad.1 = (bf16[16,48,1280]{2,1,0:T(8,128)(2,1)}, bf16[16,48,1280]{2,1,0:T(8,128)(2,1)}) custom-call(s32[3,16]{1,0:T(4,128)} %get-tuple-element.107.order, bf16[1024,768]{1,0:T(8,128)(2,1)} %bitcast.128, bf16[1024,768]{1,0:T(8,128)(2,1)} %get-tuple-element.63.q_grad, bf16[1024,768]{1,0:T(8,128)(2,1)} %get-tuple-element.64.k_grad, ...), custom_call_target="tpu_custom_call" | custom-call | flops 6000000000 | bytes 14000000 | tf_op jit(solution)/shard_map/qkv_grad/pallas_call | solution.py:616
  220.0 11.3 %down_grad.1 = (bf16[16,192,384]{2,1,0:T(8,128)(2,1)}, bf16[16,192,384]{2,1,0:T(8,128)(2,1)}) custom-call(s32[3,16]{1,0:T(4,128)} %get-tuple-element.107.order, bf16[1024,3072]{1,0:T(8,128)(2,1)} %get-tuple-element.50.active, bf16[1024,768]{1,0:T(8,128)(2,1)} %get-tuple-element.77.branch_two), custom_call_target="tpu_custom_call" | custom-call | flops 7000000000 | bytes 14000000 | tf_op jit(solution)/shard_map/down_grad/pallas_call | solution.py:441
  231.8 14.9 %up_grad.1 = (bf16[16,48,1920]{2,1,0:T(8,128)(2,1)}, bf16[16,48,1920]{2,1,0:T(8,128)(2,1)}) custom-call(s32[3,16]{1,0:T(4,128)} %get-tuple-element.107.order, bf16[1024,768]{1,0:T(8,128)(2,1)} %get-tuple-element.52.normed, bf16[1024,3072]{1,0:T(8,128)(2,1)} %get-tuple-element.74.pre_grad, bf16[1024,768]{1,0:T(8,128)(2,1)} %get-tuple-element.47.attended, ...), custom_call_target="tpu_custom_call" | custom-call | flops 8999999488 | bytes 18000000 | tf_op jit(solution)/shard_map/up_grad/pallas_call | solution.py:496
  246.7 2.7 add_convert_fusion.2
  249.4 2.0 collective-permute-start.22
  251.4 9.8 %token_grad.1 = bf16[1024,768]{1,0:T(8,128)(2,1)} custom-call(s32[3,16]{1,0:T(4,128)} %get-tuple-element.108.table, bf16[1024,768]{1,0:T(8,128)(2,1)} %get-tuple-element.63.q_grad, bf16[1024,768]{1,0:T(8,128)(2,1)} %get-tuple-element.64.k_grad, bf16[1024,768]{1,0:T(8,128)(2,1)} %get-tuple-element.65.v_grad, ...), custom_call_target="tpu_custom_call" | custom-call | flops 6000000000 | bytes 12000000 | tf_op jit(solution)/shard_map/token_grad/pallas_call | solution.py:651
  261.3 2.1 add_convert_fusion.1
  263.8 2.0 convert_add_fusion.2
  265.8 2.0 collective-permute-start.23
  268.2 1.2 copy-done.4
  269.5 1.5 collective-permute-start.29
  271.0 9.1 %collective-permute-done.23 = bf16[4,48,1280]{2,1,0:T(8,128)(2,1)S(1)} collective-permute-done((bf16[4,48,1280]{2,1,0:T(8,128)(2,1)S(1)}, bf16[4,48,1280]{2,1,0:T(8,128)(2,1)S(1)}, u32[]{:S(2)}, u32[]{:S(2)}) %collective-permute-start.23) | collective-permute-done | bytes 491552 | tf_op jit(solution)/shard_map/ppermute | solution.py:72
  280.3 2.4 collective-permute-start.26
  282.7 1.1 collective-permute-start.25
  283.8 1.1 collective-permute-done.37
  284.9 1.8 convert_add_fusion.1
  286.7 1.0 slice.265
  287.7 1.5 collective-permute-start.38
  289.1 4.4 %collective-permute-done.25 = bf16[48,1280]{1,0:T(8,128)(2,1)S(1)} collective-permute-done((bf16[48,1280]{1,0:T(8,128)(2,1)S(1)}, bf16[48,1280]{1,0:T(8,128)(2,1)S(1)}, u32[]{:S(2)}, u32[]{:S(2)}) %collective-permute-start.25) | collective-permute-done | bytes 122912 | tf_op jit(solution)/shard_map/ppermute | solution.py:76
  293.7 13.3 %collective-permute-done.29 = bf16[8,48,1920]{2,1,0:T(8,128)(2,1)S(1)} collective-permute-done((bf16[8,48,1920]{2,1,0:T(8,128)(2,1)S(1)}, bf16[8,48,1920]{2,1,0:T(8,128)(2,1)S(1)}, u32[]{:S(2)}, u32[]{:S(2)}) %collective-permute-start.29) | collective-permute-done | bytes 1474592 | tf_op jit(solution)/shard_map/ppermute | solution.py:72
  307.5 0.9 slice.264
  308.4 1.5 collective-permute-start.30
  311.4 0.8 slice_reduce_fusion
  312.2 1.6 fusion.7
  313.9 1.9 collective-permute-start.41
  315.9 1.6 collective-permute-start.40
  317.4 2.8 collective-permute-done.30
  320.2 1.3 fusion.8
  321.7 1.9 collective-permute-start.33
  323.7 5.6 %collective-permute-start.32 = (bf16[48,1920]{1,0:T(8,128)(2,1)S(1)}, bf16[48,1920]{1,0:T(8,128)(2,1)S(1)}, u32[]{:S(2)}, u32[]{:S(2)}) collective-permute-start(bf16[48,1920]{1,0:T(8,128)(2,1)S(1)} %get-tuple-element.96), channel_id=1, source_target_pairs={{0,8},{1,9},{2,10},{3,11},{4,12},{5,13},{6,14},{7,15},{8,0},{9,1},... | collective-permute-start | bytes 552968 | tf_op jit(solution)/shard_map/ppermute | solution.py:76
  329.3 10.1 %collective-permute-done.40 = bf16[192,384]{1,0:T(8,128)(2,1)S(1)} collective-permute-done((bf16[192,384]{1,0:T(8,128)(2,1)S(1)}, bf16[192,384]{1,0:T(8,128)(2,1)S(1)}, u32[]{:S(2)}, u32[]{:S(2)}) %collective-permute-start.40) | collective-permute-done | bytes 147488 | tf_op jit(solution)/shard_map/ppermute | solution.py:76
  339.6 7.0 %collective-permute-done.32 = bf16[48,1920]{1,0:T(8,128)(2,1)S(1)} collective-permute-done((bf16[48,1920]{1,0:T(8,128)(2,1)S(1)}, bf16[48,1920]{1,0:T(8,128)(2,1)S(1)}, u32[]{:S(2)}, u32[]{:S(2)}) %collective-permute-start.32) | collective-permute-done | bytes 184352 | tf_op jit(solution)/shard_map/ppermute | solution.py:76
  346.9 0.8 maximum_select_fusion.2
  348.2 0.9 maximum_select_fusion.1
  349.7 0.9 maximum_select_fusion
  (119 shorter events, 14.9 us)
Async XLA Ops:
  0.6 9.9 %copy-start = (bf16[48,3072]{1,0:T(8,128)(2,1)S(1)}, bf16[48,3072]{1,0:T(8,128)(2,1)}, u32[]{:S(2)}) copy-start(bf16[48,3072]{1,0:T(8,128)(2,1)} %param.23) | copy-start | bytes 884740
  0.7 15.0 %copy-start.8 = (bf16[192,768]{1,0:T(8,128)(2,1)S(1)}, bf16[192,768]{1,0:T(8,128)(2,1)}, u32[]{:S(2)}) copy-start(bf16[192,768]{1,0:T(8,128)(2,1)} %param.25) | copy-start | bytes 884740
  4.0 13.0 %collective-permute-start.1 = (bf16[48,1280]{1,0:T(8,128)(2,1)S(1)}, bf16[48,1280]{1,0:T(8,128)(2,1)S(1)}, u32[]{:S(2)}, u32[]{:S(2)}) collective-permute-start(bf16[48,1280]{1,0:T(8,128)(2,1)S(1)} %get-tuple-element.106), channel_id=1, source_target_pairs={{0,8},{1,9},{2,10},{3,11},{4,12},{5,13},{6,14},{7,15},{8,0},{9,1},... | collective-permute-start | bytes 368648 | tf_op jit(solution)/shard_map/ppermute | solution.py:76
  8.1 8.3 %collective-permute-start = (bf16[48,1280]{1,0:T(8,128)(2,1)S(1)}, bf16[48,1280]{1,0:T(8,128)(2,1)S(1)}, u32[]{:S(2)}, u32[]{:S(2)}) collective-permute-start(bf16[48,1280]{1,0:T(8,128)(2,1)S(1)} %get-tuple-element.106), channel_id=1, source_target_pairs={{0,4},{1,5},{2,6},{3,7},{4,0},{5,1},{6,2},{7,3},{8,12},{9,13},{10,... | collective-permute-start | bytes 368648 | tf_op jit(solution)/shard_map/ppermute | solution.py:76
  9.7 10.1 %collective-permute-start.2 = (bf16[48,1280]{1,0:T(8,128)(2,1)S(1)}, bf16[48,1280]{1,0:T(8,128)(2,1)S(1)}, u32[]{:S(2)}, u32[]{:S(2)}) collective-permute-start(bf16[48,1280]{1,0:T(8,128)(2,1)S(1)} %get-tuple-element.106), channel_id=1, source_target_pairs={{0,12},{1,13},{2,14},{3,15},{4,8},{5,9},{6,10},{7,11},{8,4},{9,5},... | collective-permute-start | bytes 368648 | tf_op jit(solution)/shard_map/ppermute | solution.py:76
  10.6 36.9 %collective-permute-start.8 = (bf16[48,1920]{1,0:T(8,128)(2,1)S(1)}, bf16[48,1920]{1,0:T(8,128)(2,1)S(1)}, u32[]{:S(2)}, u32[]{:S(2)}) collective-permute-start(bf16[48,1920]{1,0:T(8,128)(2,1)S(1)} %get-tuple-element.104), channel_id=1, source_target_pairs={{0,8},{1,9},{2,10},{3,11},{4,12},{5,13},{6,14},{7,15},{8,0},{9,1},... | collective-permute-start | bytes 552968 | tf_op jit(solution)/shard_map/ppermute | solution.py:76
  12.5 34.9 %collective-permute-start.7 = (bf16[48,1920]{1,0:T(8,128)(2,1)S(1)}, bf16[48,1920]{1,0:T(8,128)(2,1)S(1)}, u32[]{:S(2)}, u32[]{:S(2)}) collective-permute-start(bf16[48,1920]{1,0:T(8,128)(2,1)S(1)} %get-tuple-element.104), channel_id=1, source_target_pairs={{0,4},{1,5},{2,6},{3,7},{4,0},{5,1},{6,2},{7,3},{8,12},{9,13},{10,... | collective-permute-start | bytes 552968 | tf_op jit(solution)/shard_map/ppermute | solution.py:76
  16.4 13.6 %collective-permute-start.16 = (bf16[192,384]{1,0:T(8,128)(2,1)S(1)}, bf16[192,384]{1,0:T(8,128)(2,1)S(1)}, u32[]{:S(2)}, u32[]{:S(2)}) collective-permute-start(bf16[192,384]{1,0:T(8,128)(2,1)S(1)} %get-tuple-element.93), channel_id=1, source_target_pairs={{0,12},{1,13},{2,14},{3,15},{4,8},{5,9},{6,10},{7,11},{8,4},{9,5},... | collective-permute-start | bytes 442376 | tf_op jit(solution)/shard_map/ppermute | solution.py:76
  17.1 26.8 %collective-permute-start.15 = (bf16[192,384]{1,0:T(8,128)(2,1)S(1)}, bf16[192,384]{1,0:T(8,128)(2,1)S(1)}, u32[]{:S(2)}, u32[]{:S(2)}) collective-permute-start(bf16[192,384]{1,0:T(8,128)(2,1)S(1)} %get-tuple-element.93), channel_id=1, source_target_pairs={{0,8},{1,9},{2,10},{3,11},{4,12},{5,13},{6,14},{7,15},{8,0},{9,1},... | collective-permute-start | bytes 442376 | tf_op jit(solution)/shard_map/ppermute | solution.py:76
  19.8 25.7 %collective-permute-start.14 = (bf16[192,384]{1,0:T(8,128)(2,1)S(1)}, bf16[192,384]{1,0:T(8,128)(2,1)S(1)}, u32[]{:S(2)}, u32[]{:S(2)}) collective-permute-start(bf16[192,384]{1,0:T(8,128)(2,1)S(1)} %get-tuple-element.93), channel_id=1, source_target_pairs={{0,4},{1,5},{2,6},{3,7},{4,0},{5,1},{6,2},{7,3},{8,12},{9,13},{10,... | collective-permute-start | bytes 442376 | tf_op jit(solution)/shard_map/ppermute | solution.py:76
  30.0 17.4 %collective-permute-start.9 = (bf16[48,1920]{1,0:T(8,128)(2,1)S(1)}, bf16[48,1920]{1,0:T(8,128)(2,1)S(1)}, u32[]{:S(2)}, u32[]{:S(2)}) collective-permute-start(bf16[48,1920]{1,0:T(8,128)(2,1)S(1)} %get-tuple-element.104), channel_id=1, source_target_pairs={{0,12},{1,13},{2,14},{3,15},{4,8},{5,9},{6,10},{7,11},{8,4},{9,5},... | collective-permute-start | bytes 552968 | tf_op jit(solution)/shard_map/ppermute | solution.py:76
  43.9 8.8 %collective-permute-start.3 = (bf16[4,48,1280]{2,1,0:T(8,128)(2,1)S(1)}, bf16[4,48,1280]{2,1,0:T(8,128)(2,1)S(1)}, u32[]{:S(2)}, u32[]{:S(2)}) collective-permute-start(bf16[4,48,1280]{2,1,0:T(8,128)(2,1)S(1)} %pad_maximum_fusion.2), channel_id=1, source_target_pairs={{0,1},{1,0},{2,3},{3,2},{4,5},{5,4},{6,7},{7,6},{8,9},{9,8},{10,11... | collective-permute-start | bytes 1474568 | tf_op jit(solution)/shard_map/ppermute | solution.py:72
  45.5 36.2 %collective-permute-start.17 = (bf16[4,192,384]{2,1,0:T(8,128)(2,1)S(1)}, bf16[4,192,384]{2,1,0:T(8,128)(2,1)S(1)}, u32[]{:S(2)}, u32[]{:S(2)}) collective-permute-start(bf16[4,192,384]{2,1,0:T(8,128)(2,1)S(1)} %pad_maximum_fusion.1), channel_id=1, source_target_pairs={{0,1},{1,0},{2,3},{3,2},{4,5},{5,4},{6,7},{7,6},{8,9},{9,8},{10,11... | collective-permute-start | bytes 1769480 | tf_op jit(solution)/shard_map/ppermute | solution.py:72
  47.6 31.3 %collective-permute-start.10 = (bf16[4,48,1920]{2,1,0:T(8,128)(2,1)S(1)}, bf16[4,48,1920]{2,1,0:T(8,128)(2,1)S(1)}, u32[]{:S(2)}, u32[]{:S(2)}) collective-permute-start(bf16[4,48,1920]{2,1,0:T(8,128)(2,1)S(1)} %pad_maximum_fusion), channel_id=1, source_target_pairs={{0,1},{1,0},{2,3},{3,2},{4,5},{5,4},{6,7},{7,6},{8,9},{9,8},{10,11... | collective-permute-start | bytes 2211848 | tf_op jit(solution)/shard_map/ppermute | solution.py:72
  53.6 29.2 %collective-permute-start.4 = (bf16[8,48,1280]{2,1,0:T(8,128)(2,1)}, bf16[8,48,1280]{2,1,0:T(8,128)(2,1)}, u32[]{:S(2)}, u32[]{:S(2)}) collective-permute-start(bf16[8,48,1280]{2,1,0:T(8,128)(2,1)} %constant_dynamic-update-slice_fusion.s0), channel_id=1, source_target_pairs={{0,2},{1,3},{2,0},{3,1},{4,6},{5,7},{6,4},{7,5},{8,10},{9,11},{10,... | collective-permute-start | bytes 2949128 | tf_op jit(solution)/shard_map/ppermute | solution.py:72
  78.9 55.3 %copy-start.9 = (bf16[8,48,1920]{2,1,0:T(8,128)(2,1)}, bf16[8,48,1920]{2,1,0:T(8,128)(2,1)S(1)}, u32[]{:S(2)}) copy-start(bf16[8,48,1920]{2,1,0:T(8,128)(2,1)S(1)} %constant_dynamic-update-slice_fusion.5.s0.u0) | copy-start | bytes 4423684
  78.9 32.2 %collective-permute-start.11 = (bf16[8,48,1920]{2,1,0:T(8,128)(2,1)S(1)}, bf16[8,48,1920]{2,1,0:T(8,128)(2,1)S(1)}, u32[]{:S(2)}, u32[]{:S(2)}) collective-permute-start(bf16[8,48,1920]{2,1,0:T(8,128)(2,1)S(1)} %constant_dynamic-update-slice_fusion.5.s0.u0), channel_id=1, source_target_pairs={{0,2},{1,3},{2,0},{3,1},{4,6},{5,7},{6,4},{7,5},{8,10},{9,11},{10,... | collective-permute-start | bytes 4423688 | tf_op jit(solution)/shard_map/ppermute | solution.py:72
  82.6 28.5 %collective-permute-start.18 = (bf16[8,192,384]{2,1,0:T(8,128)(2,1)}, bf16[8,192,384]{2,1,0:T(8,128)(2,1)}, u32[]{:S(2)}, u32[]{:S(2)}) collective-permute-start(bf16[8,192,384]{2,1,0:T(8,128)(2,1)} %constant_dynamic-update-slice_fusion.10.d0), channel_id=1, source_target_pairs={{0,2},{1,3},{2,0},{3,1},{4,6},{5,7},{6,4},{7,5},{8,10},{9,11},{10,... | collective-permute-start | bytes 3538952 | tf_op jit(solution)/shard_map/ppermute | solution.py:72
  82.7 3.9 %collective-permute-start.5 = (bf16[8,48,1280]{2,1,0:T(8,128)(2,1)}, bf16[8,48,1280]{2,1,0:T(8,128)(2,1)}, u32[]{:S(2)}, u32[]{:S(2)}) collective-permute-start(bf16[8,48,1280]{2,1,0:T(8,128)(2,1)} %constant_dynamic-update-slice_fusion.s0), channel_id=1, source_target_pairs={{0,16},{16,0},{1,17},{17,1},{2,18},{18,2},{3,19},{19,3},{4,20},{20... | collective-permute-start | bytes 2949128 | tf_op jit(solution)/shard_map/ppermute | solution.py:66
  82.8 28.9 %collective-permute-start.6 = (bf16[8,48,1280]{2,1,0:T(8,128)(2,1)}, bf16[8,48,1280]{2,1,0:T(8,128)(2,1)}, u32[]{:S(2)}, u32[]{:S(2)}) collective-permute-start(bf16[8,48,1280]{2,1,0:T(8,128)(2,1)} %collective-permute-done.4.s1), channel_id=1, source_target_pairs={{0,16},{16,0},{1,17},{17,1},{2,18},{18,2},{3,19},{19,3},{4,20},{20... | collective-permute-start | bytes 2949128 | tf_op jit(solution)/shard_map/ppermute | solution.py:66
  86.7 66.7 %collective-permute-start.19 = (bf16[8,192,384]{2,1,0:T(8,128)(2,1)}, bf16[8,192,384]{2,1,0:T(8,128)(2,1)}, u32[]{:S(2)}, u32[]{:S(2)}) collective-permute-start(bf16[8,192,384]{2,1,0:T(8,128)(2,1)} %constant_dynamic-update-slice_fusion.10.d0), channel_id=1, source_target_pairs={{0,16},{16,0},{1,17},{17,1},{2,18},{18,2},{3,19},{19,3},{4,20},{20... | collective-permute-start | bytes 3538952 | tf_op jit(solution)/shard_map/ppermute | solution.py:66
  86.7 47.6 %collective-permute-start.12 = (bf16[8,48,1920]{2,1,0:T(8,128)(2,1)S(1)}, bf16[8,48,1920]{2,1,0:T(8,128)(2,1)}, u32[]{:S(2)}, u32[]{:S(2)}) collective-permute-start(bf16[8,48,1920]{2,1,0:T(8,128)(2,1)S(1)} %constant_dynamic-update-slice_fusion.5.s0.u0), channel_id=1, source_target_pairs={{0,16},{16,0},{1,17},{17,1},{2,18},{18,2},{3,19},{19,3},{4,20},{20... | collective-permute-start | bytes 4423688 | tf_op jit(solution)/shard_map/ppermute | solution.py:66
  111.1 42.2 %collective-permute-start.20 = (bf16[8,192,384]{2,1,0:T(8,128)(2,1)}, bf16[8,192,384]{2,1,0:T(8,128)(2,1)}, u32[]{:S(2)}, u32[]{:S(2)}) collective-permute-start(bf16[8,192,384]{2,1,0:T(8,128)(2,1)} %collective-permute-done.18.d1), channel_id=1, source_target_pairs={{0,16},{16,0},{1,17},{17,1},{2,18},{18,2},{3,19},{19,3},{4,20},{20... | collective-permute-start | bytes 3538952 | tf_op jit(solution)/shard_map/ppermute | solution.py:66
  111.2 23.1 %copy-start.10 = (bf16[8,48,1920]{2,1,0:T(8,128)(2,1)}, bf16[8,48,1920]{2,1,0:T(8,128)(2,1)S(1)}, u32[]{:S(2)}) copy-start(bf16[8,48,1920]{2,1,0:T(8,128)(2,1)S(1)} %collective-permute-done.11.s1.u1) | copy-start | bytes 4423684
  111.2 23.1 %collective-permute-start.13 = (bf16[8,48,1920]{2,1,0:T(8,128)(2,1)S(1)}, bf16[8,48,1920]{2,1,0:T(8,128)(2,1)}, u32[]{:S(2)}, u32[]{:S(2)}) collective-permute-start(bf16[8,48,1920]{2,1,0:T(8,128)(2,1)S(1)} %collective-permute-done.11.s1.u1), channel_id=1, source_target_pairs={{0,16},{16,0},{1,17},{17,1},{2,18},{18,2},{3,19},{19,3},{4,20},{20... | collective-permute-start | bytes 4423688 | tf_op jit(solution)/shard_map/ppermute | solution.py:66
  220.0 26.7 %collective-permute-start.21 = (bf16[16,48,1280]{2,1,0:T(8,128)(2,1)}, bf16[16,48,1280]{2,1,0:T(8,128)(2,1)}, u32[]{:S(2)}, u32[]{:S(2)}) collective-permute-start(bf16[16,48,1280]{2,1,0:T(8,128)(2,1)} %get-tuple-element.73), channel_id=1, source_target_pairs={{0,16},{16,0},{1,17},{17,1},{2,18},{18,2},{3,19},{19,3},{4,20},{20... | collective-permute-start | bytes 5898248 | tf_op jit(solution)/shard_map/ppermute | solution.py:66
  231.3 30.0 %collective-permute-start.36 = (bf16[16,192,384]{2,1,0:T(8,128)(2,1)}, bf16[16,192,384]{2,1,0:T(8,128)(2,1)}, u32[]{:S(2)}, u32[]{:S(2)}) collective-permute-start(bf16[16,192,384]{2,1,0:T(8,128)(2,1)} %get-tuple-element.79), channel_id=1, source_target_pairs={{0,16},{16,0},{1,17},{17,1},{2,18},{18,2},{3,19},{19,3},{4,20},{20... | collective-permute-start | bytes 7077896 | tf_op jit(solution)/shard_map/ppermute | solution.py:66
  246.6 21.2 %collective-permute-start.28 = (bf16[16,48,1920]{2,1,0:T(8,128)(2,1)}, bf16[16,48,1920]{2,1,0:T(8,128)(2,1)S(1)}, u32[]{:S(2)}, u32[]{:S(2)}) collective-permute-start(bf16[16,48,1920]{2,1,0:T(8,128)(2,1)} %get-tuple-element.76), channel_id=1, source_target_pairs={{0,16},{16,0},{1,17},{17,1},{2,18},{18,2},{3,19},{19,3},{4,20},{20... | collective-permute-start | bytes 8847368 | tf_op jit(solution)/shard_map/ppermute | solution.py:66
  249.4 14.4 %collective-permute-start.22 = (bf16[8,48,1280]{2,1,0:T(8,128)(2,1)}, bf16[8,48,1280]{2,1,0:T(8,128)(2,1)}, u32[]{:S(2)}, u32[]{:S(2)}) collective-permute-start(bf16[8,48,1280]{2,1,0:T(8,128)(2,1)} %add_convert_fusion.2), channel_id=1, source_target_pairs={{0,2},{1,3},{2,0},{3,1},{4,6},{5,7},{6,4},{7,5},{8,10},{9,11},{10,... | collective-permute-start | bytes 2949128 | tf_op jit(solution)/shard_map/ppermute | solution.py:72
  261.3 2.5 copy-start.7
  263.3 21.5 %collective-permute-start.37 = (bf16[8,192,384]{2,1,0:T(8,128)(2,1)S(1)}, bf16[8,192,384]{2,1,0:T(8,128)(2,1)S(1)}, u32[]{:S(2)}, u32[]{:S(2)}) collective-permute-start(bf16[8,192,384]{2,1,0:T(8,128)(2,1)S(1)} %add_convert_fusion.1), channel_id=1, source_target_pairs={{0,2},{1,3},{2,0},{3,1},{4,6},{5,7},{6,4},{7,5},{8,10},{9,11},{10,... | collective-permute-start | bytes 3538952 | tf_op jit(solution)/shard_map/ppermute | solution.py:72
  263.8 4.1 %copy-start.3 = (bf16[16,48,1920]{2,1,0:T(8,128)(2,1)S(1)}, bf16[16,48,1920]{2,1,0:T(8,128)(2,1)}, u32[]{:S(2)}) copy-start(bf16[16,48,1920]{2,1,0:T(8,128)(2,1)} %get-tuple-element.75) | copy-start | bytes 8847364
  265.8 14.2 %collective-permute-start.23 = (bf16[4,48,1280]{2,1,0:T(8,128)(2,1)S(1)}, bf16[4,48,1280]{2,1,0:T(8,128)(2,1)S(1)}, u32[]{:S(2)}, u32[]{:S(2)}) collective-permute-start(bf16[4,48,1280]{2,1,0:T(8,128)(2,1)S(1)} %slice.266), channel_id=1, source_target_pairs={{0,1},{1,0},{2,3},{3,2},{4,5},{5,4},{6,7},{7,6},{8,9},{9,8},{10,11... | collective-permute-start | bytes 1474568 | tf_op jit(solution)/shard_map/ppermute | solution.py:72
  267.9 1.6 copy-start.4
  269.5 15.4 %copy-start.6 = (bf16[16,192,384]{2,1,0:T(8,128)(2,1)S(1)}, bf16[16,192,384]{2,1,0:T(8,128)(2,1)}, u32[]{:S(2)}) copy-start(bf16[16,192,384]{2,1,0:T(8,128)(2,1)} %get-tuple-element.78) | copy-start | bytes 7077892
  269.5 37.5 %collective-permute-start.29 = (bf16[8,48,1920]{2,1,0:T(8,128)(2,1)S(1)}, bf16[8,48,1920]{2,1,0:T(8,128)(2,1)S(1)}, u32[]{:S(2)}, u32[]{:S(2)}) collective-permute-start(bf16[8,48,1920]{2,1,0:T(8,128)(2,1)S(1)} %add_convert_fusion), channel_id=1, source_target_pairs={{0,2},{1,3},{2,0},{3,1},{4,6},{5,7},{6,4},{7,5},{8,10},{9,11},{10,... | collective-permute-start | bytes 4423688 | tf_op jit(solution)/shard_map/ppermute | solution.py:72
  280.2 8.9 %collective-permute-start.24 = (bf16[48,1280]{1,0:T(8,128)(2,1)S(1)}, bf16[48,1280]{1,0:T(8,128)(2,1)S(1)}, u32[]{:S(2)}, u32[]{:S(2)}) collective-permute-start(bf16[48,1280]{1,0:T(8,128)(2,1)S(1)} %get-tuple-element.100), channel_id=1, source_target_pairs={{0,4},{1,5},{2,6},{3,7},{4,0},{5,1},{6,2},{7,3},{8,12},{9,13},{10,... | collective-permute-start | bytes 368648 | tf_op jit(solution)/shard_map/ppermute | solution.py:76
  280.3 8.8 %collective-permute-start.26 = (bf16[48,1280]{1,0:T(8,128)(2,1)S(1)}, bf16[48,1280]{1,0:T(8,128)(2,1)S(1)}, u32[]{:S(2)}, u32[]{:S(2)}) collective-permute-start(bf16[48,1280]{1,0:T(8,128)(2,1)S(1)} %get-tuple-element.101), channel_id=1, source_target_pairs={{0,12},{1,13},{2,14},{3,15},{4,8},{5,9},{6,10},{7,11},{8,4},{9,5},... | collective-permute-start | bytes 368648 | tf_op jit(solution)/shard_map/ppermute | solution.py:76
  282.7 10.9 %collective-permute-start.25 = (bf16[48,1280]{1,0:T(8,128)(2,1)S(1)}, bf16[48,1280]{1,0:T(8,128)(2,1)S(1)}, u32[]{:S(2)}, u32[]{:S(2)}) collective-permute-start(bf16[48,1280]{1,0:T(8,128)(2,1)S(1)} %get-tuple-element.102), channel_id=1, source_target_pairs={{0,8},{1,9},{2,10},{3,11},{4,12},{5,13},{6,14},{7,15},{8,0},{9,1},... | collective-permute-start | bytes 368648 | tf_op jit(solution)/shard_map/ppermute | solution.py:76
  284.9 22.1 %copy-start.5 = (bf16[16,48,1920]{2,1,0:T(8,128)(2,1)S(1)}, bf16[16,48,1920]{2,1,0:T(8,128)(2,1)}, u32[]{:S(2)}) copy-start(bf16[16,48,1920]{2,1,0:T(8,128)(2,1)} %copy-done.4) | copy-start | bytes 8847364
  286.7 7.0 %copy-start.2 = (f32[8,192,384]{2,1,0:T(8,128)}, f32[8,192,384]{2,1,0:T(8,128)S(1)}, u32[]{:S(2)}) copy-start(f32[8,192,384]{2,1,0:T(8,128)S(1)} %convert_add_fusion.1) | copy-start | bytes 7077892
  287.7 24.5 %collective-permute-start.38 = (bf16[4,192,384]{2,1,0:T(8,128)(2,1)}, bf16[4,192,384]{2,1,0:T(8,128)(2,1)}, u32[]{:S(2)}, u32[]{:S(2)}) collective-permute-start(bf16[4,192,384]{2,1,0:T(8,128)(2,1)} %slice.265), channel_id=1, source_target_pairs={{0,1},{1,0},{2,3},{3,2},{4,5},{5,4},{6,7},{7,6},{8,9},{9,8},{10,11... | collective-permute-start | bytes 1769480 | tf_op jit(solution)/shard_map/ppermute | solution.py:72
  308.4 11.8 %collective-permute-start.30 = (bf16[4,48,1920]{2,1,0:T(8,128)(2,1)}, bf16[4,48,1920]{2,1,0:T(8,128)(2,1)}, u32[]{:S(2)}, u32[]{:S(2)}) collective-permute-start(bf16[4,48,1920]{2,1,0:T(8,128)(2,1)} %slice.264), channel_id=1, source_target_pairs={{0,1},{1,0},{2,3},{3,2},{4,5},{5,4},{6,7},{7,6},{8,9},{9,8},{10,11... | collective-permute-start | bytes 2211848 | tf_op jit(solution)/shard_map/ppermute | solution.py:72
  311.4 35.5 %collective-permute-start.27 = (f32[48,1152]{1,0:T(8,128)S(1)}, f32[48,1152]{1,0:T(8,128)S(1)}, u32[]{:S(2)}, u32[]{:S(2)}) collective-permute-start(f32[48,1152]{1,0:T(8,128)S(1)} %slice.193), channel_id=1, source_target_pairs={{0,16},{16,0},{1,17},{17,1},{2,18},{18,2},{3,19},{19,3},{4,20},{20... | collective-permute-start | bytes 663560 | tf_op jit(solution)/shard_map/ppermute | solution.py:66
  313.9 7.8 %collective-permute-start.39 = (bf16[192,384]{1,0:T(8,128)(2,1)S(1)}, bf16[192,384]{1,0:T(8,128)(2,1)S(1)}, u32[]{:S(2)}, u32[]{:S(2)}) collective-permute-start(bf16[192,384]{1,0:T(8,128)(2,1)S(1)} %get-tuple-element.97), channel_id=1, source_target_pairs={{0,4},{1,5},{2,6},{3,7},{4,0},{5,1},{6,2},{7,3},{8,12},{9,13},{10,... | collective-permute-start | bytes 442376 | tf_op jit(solution)/shard_map/ppermute | solution.py:76
  313.9 9.8 %collective-permute-start.41 = (bf16[192,384]{1,0:T(8,128)(2,1)S(1)}, bf16[192,384]{1,0:T(8,128)(2,1)S(1)}, u32[]{:S(2)}, u32[]{:S(2)}) collective-permute-start(bf16[192,384]{1,0:T(8,128)(2,1)S(1)} %get-tuple-element.98), channel_id=1, source_target_pairs={{0,12},{1,13},{2,14},{3,15},{4,8},{5,9},{6,10},{7,11},{8,4},{9,5},... | collective-permute-start | bytes 442376 | tf_op jit(solution)/shard_map/ppermute | solution.py:76
  315.9 23.6 %collective-permute-start.40 = (bf16[192,384]{1,0:T(8,128)(2,1)S(1)}, bf16[192,384]{1,0:T(8,128)(2,1)S(1)}, u32[]{:S(2)}, u32[]{:S(2)}) collective-permute-start(bf16[192,384]{1,0:T(8,128)(2,1)S(1)} %get-tuple-element.99), channel_id=1, source_target_pairs={{0,8},{1,9},{2,10},{3,11},{4,12},{5,13},{6,14},{7,15},{8,0},{9,1},... | collective-permute-start | bytes 442376 | tf_op jit(solution)/shard_map/ppermute | solution.py:76
  321.6 18.0 %collective-permute-start.31 = (bf16[48,1920]{1,0:T(8,128)(2,1)S(1)}, bf16[48,1920]{1,0:T(8,128)(2,1)S(1)}, u32[]{:S(2)}, u32[]{:S(2)}) collective-permute-start(bf16[48,1920]{1,0:T(8,128)(2,1)S(1)} %get-tuple-element.94), channel_id=1, source_target_pairs={{0,4},{1,5},{2,6},{3,7},{4,0},{5,1},{6,2},{7,3},{8,12},{9,13},{10,... | collective-permute-start | bytes 552968 | tf_op jit(solution)/shard_map/ppermute | solution.py:76
  321.7 18.0 %collective-permute-start.33 = (bf16[48,1920]{1,0:T(8,128)(2,1)S(1)}, bf16[48,1920]{1,0:T(8,128)(2,1)S(1)}, u32[]{:S(2)}, u32[]{:S(2)}) collective-permute-start(bf16[48,1920]{1,0:T(8,128)(2,1)S(1)} %get-tuple-element.95), channel_id=1, source_target_pairs={{0,12},{1,13},{2,14},{3,15},{4,8},{5,9},{6,10},{7,11},{8,4},{9,5},... | collective-permute-start | bytes 552968 | tf_op jit(solution)/shard_map/ppermute | solution.py:76
  323.7 22.9 %collective-permute-start.32 = (bf16[48,1920]{1,0:T(8,128)(2,1)S(1)}, bf16[48,1920]{1,0:T(8,128)(2,1)S(1)}, u32[]{:S(2)}, u32[]{:S(2)}) collective-permute-start(bf16[48,1920]{1,0:T(8,128)(2,1)S(1)} %get-tuple-element.96), channel_id=1, source_target_pairs={{0,8},{1,9},{2,10},{3,11},{4,12},{5,13},{6,14},{7,15},{8,0},{9,1},... | collective-permute-start | bytes 552968 | tf_op jit(solution)/shard_map/ppermute | solution.py:76
  339.5 8.6 %collective-permute-start.42 = (f32[192,384]{1,0:T(8,128)S(1)}, f32[192,384]{1,0:T(8,128)S(1)}, u32[]{:S(2)}, u32[]{:S(2)}) collective-permute-start(f32[192,384]{1,0:T(8,128)S(1)} %fusion.1), channel_id=1, source_target_pairs={{0,16},{16,0},{1,17},{17,1},{2,18},{18,2},{3,19},{19,3},{4,20},{20... | collective-permute-start | bytes 884744 | tf_op jit(solution)/shard_map/ppermute | solution.py:66
  346.8 3.0 collective-permute-start.35
  346.9 3.8 %copy-start.1 = (bf16[48,3072]{1,0:T(8,128)(2,1)S(1)}, bf16[48,3072]{1,0:T(8,128)(2,1)}, u32[]{:S(2)}) copy-start(bf16[48,3072]{1,0:T(8,128)(2,1)} %param.23) | copy-start | bytes 884740
  347.7 1.4 collective-permute-start.34
